TPU v7x, 128 devices: a whole 4x4x4 slice. The times are simulated.
128 devices in a mesh: segment: 4 (over z), blk: 32 (over y, x, core).
Axes of the slice: x: 4, y: 4, z: 4, core: 2. Of those that a mesh axis runs over, the one named last changes fastest.
Arguments:
- tokens: bfloat16 [256, 16384], P(None, 'blk'), may hold values from -6 to 6
- cotangent: bfloat16 [256, 16384], P(None, 'blk'), may hold values from -6 to 6
- first_factor: bfloat16 [4, 64, 256, 256], P('segment', 'blk'), may hold values from -0.375 to 0.375
- second_factor: bfloat16 [4, 64, 256, 1024], P('segment', 'blk'), may hold values from -0.375 to 0.375
- third_factor: bfloat16 [4, 64, 1024, 1024], P('segment', 'blk'), may hold values from -0.1875 to 0.1875
- fourth_factor: bfloat16 [4, 64, 1024, 256], P('segment', 'blk'), may hold values from -0.1875 to 0.1875
Outputs:
- segment_outputs: bfloat16 [4, 256, 16384], P('segment', None, 'blk')
- input_grads: bfloat16 [4, 256, 16384], P('segment', None, 'blk')
- first_grad: bfloat16 [4, 64, 256, 256], P('segment', 'blk')
- second_grad: bfloat16 [4, 64, 256, 1024], P('segment', 'blk')
- third_grad: bfloat16 [4, 64, 1024, 1024], P('segment', 'blk')
- fourth_grad: bfloat16 [4, 64, 1024, 256], P('segment', 'blk')
All inputs are finite; a program needn't handle non-finite values.
Results may differ from a plain program's by a relative error of at most 0.035.
Values may be sent and summed in bfloat16 or wider, within the bound.
No kernel may reach another device: no remote copies, remote signals or barrier semaphores. Data moves between devices by JAX's collectives and lax.ppermute only.
A program may use at most 128 MiB of HBM per device.

v0:
```python
import jax
import jax.numpy as jnp
from jax import lax
from jax.sharding import PartitionSpec as P

MB_TOK = 128


def shifted(block, axis, distance):
    devices = range(lax.axis_size(axis))
    route = [(i - distance, i) for i in devices if i - distance in devices]
    return lax.ppermute(block, axis, route)


def forward_layer(hidden_in, first, second_view, third, fourth_view):
    local_blocks = first.shape[0]
    blocks = second_view.shape[1]
    inner_first = second_view.shape[2]
    inner_second = fourth_view.shape[2]
    mixed = jnp.einsum("kit,kij->kjt", hidden_in, first, preferred_element_type=jnp.float32).astype(
        jnp.bfloat16
    )
    arrived = lax.all_to_all(mixed, "blk", split_axis=1, concat_axis=0, tiled=True)
    grouped = arrived.reshape(blocks, local_blocks, inner_first, arrived.shape[2])
    pre_part = jnp.einsum(
        "kgct,gkcm->gmt", grouped, second_view, preferred_element_type=jnp.float32
    )
    arrived_first = arrived
    pre_act = pre_part.astype(jnp.bfloat16)
    activated = jax.nn.gelu(pre_act.astype(jnp.float32)).astype(jnp.bfloat16)
    spread = jnp.einsum(
        "gmt,gmn->gnt", activated, third, preferred_element_type=jnp.float32
    ).astype(jnp.bfloat16)
    arrived = lax.all_to_all(spread, "blk", split_axis=1, concat_axis=0, tiled=True)
    grouped = arrived.reshape(blocks, local_blocks, inner_second, arrived.shape[2])
    result = jnp.einsum("gkct,kgco->kot", grouped, fourth_view, preferred_element_type=jnp.float32)
    output = (hidden_in.astype(jnp.float32) + result).astype(jnp.bfloat16)
    return (output, (arrived_first, pre_act, activated, arrived))


def backward_layer(hidden_in, upstream, saved, first, second_view, third, fourth_view):
    arrived_first, pre_act, activated, arrived_second = saved
    local_blocks = first.shape[0]
    blocks = second_view.shape[1]
    inner_first = second_view.shape[2]
    inner_second = fourth_view.shape[2]
    count = hidden_in.shape[2]
    grouped_second = arrived_second.reshape(blocks, local_blocks, inner_second, count)
    grad_fourth = jnp.einsum(
        "gkct,kot->kgco", grouped_second, upstream, preferred_element_type=jnp.float32
    )
    back_spread = jnp.einsum(
        "kot,kgco->gkct", upstream, fourth_view, preferred_element_type=jnp.float32
    )
    back_spread = back_spread.astype(jnp.bfloat16).reshape(
        blocks, local_blocks * inner_second, count
    )
    grad_spread = lax.all_to_all(back_spread, "blk", split_axis=0, concat_axis=1, tiled=True)
    grad_third = jnp.einsum(
        "gmt,gnt->gmn", activated, grad_spread, preferred_element_type=jnp.float32
    )
    grad_act = jnp.einsum("gnt,gmn->gmt", grad_spread, third, preferred_element_type=jnp.float32)
    unused, gelu_back = jax.vjp(jax.nn.gelu, pre_act.astype(jnp.float32))
    grad_pre = gelu_back(grad_act)[0].astype(jnp.bfloat16)
    grouped_first = arrived_first.reshape(blocks, local_blocks, inner_first, count)
    grad_second = jnp.einsum(
        "kgct,gmt->gkcm", grouped_first, grad_pre, preferred_element_type=jnp.float32
    )
    back_mix = jnp.einsum(
        "gmt,gkcm->kgct", grad_pre, second_view, preferred_element_type=jnp.float32
    )
    back_mix = back_mix.astype(jnp.bfloat16).reshape(blocks, local_blocks * inner_first, count)
    grad_mixed = lax.all_to_all(back_mix, "blk", split_axis=0, concat_axis=1, tiled=True)
    grad_first = jnp.einsum(
        "kit,kjt->kij", hidden_in, grad_mixed, preferred_element_type=jnp.float32
    )
    back_in = jnp.einsum("kjt,kij->kit", grad_mixed, first, preferred_element_type=jnp.float32)
    grad_in = (upstream.astype(jnp.float32) + back_in).astype(jnp.bfloat16)
    return (grad_in, (grad_first, grad_second, grad_third, grad_fourth))


def shards(tokens, cotangent, first_factor, second_factor, third_factor, fourth_factor):
    segments = lax.axis_size("segment")
    position = lax.axis_index("segment")
    first = first_factor[0]
    local_blocks = first.shape[0]
    width_block = first.shape[1]
    blocks = local_blocks * lax.axis_size("blk")
    hidden_block = third_factor.shape[2]
    inner_first = width_block // blocks
    inner_second = hidden_block // blocks
    second_view = second_factor[0].reshape(local_blocks, blocks, inner_first, hidden_block)
    third = third_factor[0]
    fourth_view = fourth_factor[0].reshape(local_blocks, blocks, inner_second, width_block)
    total = tokens.shape[0]
    micro = total // MB_TOK
    steps = micro + segments - 1
    entry = tokens.reshape(total, local_blocks, width_block).transpose(1, 2, 0)
    returning = cotangent.reshape(total, local_blocks, width_block).transpose(1, 2, 0)
    blank = jnp.zeros((local_blocks, width_block, MB_TOK), jnp.bfloat16)
    layer_weights = (first, second_view, third, fourth_view)

    def locate(step, lag):
        offset = step - lag
        valid = (offset >= 0) & (offset < micro)
        index = jnp.clip(offset, 0, micro - 1)
        return (valid, index)

    def write(buffer, value, valid, start):
        current = lax.dynamic_slice_in_dim(buffer, start, MB_TOK, 2)
        return lax.dynamic_update_slice_in_dim(buffer, jnp.where(valid, value, current), start, 2)

    store = ()

    def forward_step(step, carry):
        incoming, inputs_kept, outputs_kept, kept = carry
        valid, index = locate(step, position)
        start = index * MB_TOK
        first_rows = lax.dynamic_slice_in_dim(entry, start, MB_TOK, 2)
        current = jnp.where(position == 0, first_rows, incoming)
        output, saved = forward_layer(current, *layer_weights)
        inputs_kept = write(inputs_kept, current, valid, start)
        outputs_kept = write(outputs_kept, output, valid, start)
        incoming = shifted(output, "segment", 1)
        return (incoming, inputs_kept, outputs_kept, kept)

    start_carry = (blank, jnp.zeros_like(entry), jnp.zeros_like(entry), store)
    unused, inputs_kept, outputs_kept, store = lax.fori_loop(0, steps, forward_step, start_carry)

    def backward_step(step, carry):
        incoming, grads_kept, totals = carry
        valid, index = locate(step, segments - 1 - position)
        start = index * MB_TOK
        current = lax.dynamic_slice_in_dim(inputs_kept, start, MB_TOK, 2)
        last_rows = lax.dynamic_slice_in_dim(returning, start, MB_TOK, 2)
        upstream = jnp.where(position == segments - 1, last_rows, incoming)
        saved = forward_layer(current, *layer_weights)[1]
        grad_in, terms = backward_layer(current, upstream, saved, *layer_weights)
        factor = valid.astype(jnp.float32)
        totals = tuple((accum + factor * term for accum, term in zip(totals, terms)))
        grads_kept = write(grads_kept, grad_in, valid, start)
        incoming = shifted(grad_in, "segment", -1)
        return (incoming, grads_kept, totals)

    totals = (
        jnp.zeros((local_blocks, width_block, width_block), jnp.float32),
        jnp.zeros((local_blocks, blocks, inner_first, hidden_block), jnp.float32),
        jnp.zeros((local_blocks, hidden_block, hidden_block), jnp.float32),
        jnp.zeros((local_blocks, blocks, inner_second, width_block), jnp.float32),
    )
    unused, grads_kept, totals = lax.fori_loop(
        0, steps, backward_step, (blank, jnp.zeros_like(entry), totals)
    )
    segment_outputs = outputs_kept.transpose(2, 0, 1).reshape(total, local_blocks * width_block)[
        None
    ]
    input_grads = grads_kept.transpose(2, 0, 1).reshape(total, local_blocks * width_block)[None]
    first_grad = totals[0].astype(jnp.bfloat16)[None]
    second_grad = (
        totals[1].reshape(local_blocks, width_block, hidden_block).astype(jnp.bfloat16)[None]
    )
    third_grad = totals[2].astype(jnp.bfloat16)[None]
    fourth_grad = (
        totals[3].reshape(local_blocks, hidden_block, width_block).astype(jnp.bfloat16)[None]
    )
    return (segment_outputs, input_grads, first_grad, second_grad, third_grad, fourth_grad)


def solution(mesh):
    placed = (
        P(None, "blk"),
        P(None, "blk"),
        P("segment", "blk", None, None),
        P("segment", "blk", None, None),
        P("segment", "blk", None, None),
        P("segment", "blk", None, None),
    )
    return jax.shard_map(
        shards,
        mesh=mesh,
        in_specs=placed,
        out_specs=(
            P("segment", None, "blk"),
            P("segment", None, "blk"),
            P("segment", "blk", None, None),
            P("segment", "blk", None, None),
            P("segment", "blk", None, None),
            P("segment", "blk", None, None),
        ),
        check_vma=False,
    )
```

profile of v0, /device:TPU:1, one launch (start us, length us, event | category | flops | bytes accessed | tf_op | source)
XLA Modules:
  0.0 600.8 jit_solution(71045533582633132)
XLA Ops:
  8.8 212.7 %while.44 = (s32[]{:T(128)}, bf16[2,256,128]{1,2,0:T(8,128)(2,1)S(1)}, bf16[2,256,256]{1,2,0:T(8,128)(2,1)S(1)}, bf16[2,256,256]{1,2,0:T(8,128)(2,1)S(1)}, pred[...) while((s32[]{:T(128)}, ...), condition=%wide.region_1.2_spmd, body=%wide.region_0.1_spmd.sunk | while | flops 842465280 | bytes 15466803 | solution.py:128
  10.3 16.0 %all_to_all.238 = bf16[2,256,128]{2,0,1:T(2,128)(2,1)S(1)} all-to-all(bf16[2,256,128]{2,0,1:T(2,128)(2,1)S(1)} %copy.185), channel_id=1, replica_groups=mesh['segment'=4,'blk'=32] {'blk'}, dimensions={1} | all-to-all | bytes 262144 | tf_op jit(solution)/shard_map/while/body/eval_jaxpr/all_to_all | solution.py:23
  31.9 15.2 %all_to_all.239 = bf16[2,1024,128]{2,0,1:T(2,128)(2,1)S(1)} all-to-all(bf16[2,1024,128]{2,0,1:T(2,128)(2,1)S(1)} %copy.188), channel_id=1, replica_groups=mesh['segment'=4,'blk'=32] {'blk'}, dimensions={1} | all-to-all | bytes 1048576 | tf_op jit(solution)/shard_map/while/body/eval_jaxpr/all_to_all | solution.py:34
  55.5 12.1 %all_to_all.238 = bf16[2,256,128]{2,0,1:T(2,128)(2,1)S(1)} all-to-all(bf16[2,256,128]{2,0,1:T(2,128)(2,1)S(1)} %copy.185), channel_id=1, replica_groups=mesh['segment'=4,'blk'=32] {'blk'}, dimensions={1} | all-to-all | bytes 262144 | tf_op jit(solution)/shard_map/while/body/eval_jaxpr/all_to_all | solution.py:23
  73.2 15.2 %all_to_all.239 = bf16[2,1024,128]{2,0,1:T(2,128)(2,1)S(1)} all-to-all(bf16[2,1024,128]{2,0,1:T(2,128)(2,1)S(1)} %copy.188), channel_id=1, replica_groups=mesh['segment'=4,'blk'=32] {'blk'}, dimensions={1} | all-to-all | bytes 1048576 | tf_op jit(solution)/shard_map/while/body/eval_jaxpr/all_to_all | solution.py:34
  97.4 12.1 %all_to_all.238 = bf16[2,256,128]{2,0,1:T(2,128)(2,1)S(1)} all-to-all(bf16[2,256,128]{2,0,1:T(2,128)(2,1)S(1)} %copy.185), channel_id=1, replica_groups=mesh['segment'=4,'blk'=32] {'blk'}, dimensions={1} | all-to-all | bytes 262144 | tf_op jit(solution)/shard_map/while/body/eval_jaxpr/all_to_all | solution.py:23
  115.1 15.2 %all_to_all.239 = bf16[2,1024,128]{2,0,1:T(2,128)(2,1)S(1)} all-to-all(bf16[2,1024,128]{2,0,1:T(2,128)(2,1)S(1)} %copy.188), channel_id=1, replica_groups=mesh['segment'=4,'blk'=32] {'blk'}, dimensions={1} | all-to-all | bytes 1048576 | tf_op jit(solution)/shard_map/while/body/eval_jaxpr/all_to_all | solution.py:34
  139.2 12.1 %all_to_all.238 = bf16[2,256,128]{2,0,1:T(2,128)(2,1)S(1)} all-to-all(bf16[2,256,128]{2,0,1:T(2,128)(2,1)S(1)} %copy.185), channel_id=1, replica_groups=mesh['segment'=4,'blk'=32] {'blk'}, dimensions={1} | all-to-all | bytes 262144 | tf_op jit(solution)/shard_map/while/body/eval_jaxpr/all_to_all | solution.py:23
  157.0 15.2 %all_to_all.239 = bf16[2,1024,128]{2,0,1:T(2,128)(2,1)S(1)} all-to-all(bf16[2,1024,128]{2,0,1:T(2,128)(2,1)S(1)} %copy.188), channel_id=1, replica_groups=mesh['segment'=4,'blk'=32] {'blk'}, dimensions={1} | all-to-all | bytes 1048576 | tf_op jit(solution)/shard_map/while/body/eval_jaxpr/all_to_all | solution.py:34
  181.1 12.1 %all_to_all.238 = bf16[2,256,128]{2,0,1:T(2,128)(2,1)S(1)} all-to-all(bf16[2,256,128]{2,0,1:T(2,128)(2,1)S(1)} %copy.185), channel_id=1, replica_groups=mesh['segment'=4,'blk'=32] {'blk'}, dimensions={1} | all-to-all | bytes 262144 | tf_op jit(solution)/shard_map/while/body/eval_jaxpr/all_to_all | solution.py:23
  198.8 15.2 %all_to_all.239 = bf16[2,1024,128]{2,0,1:T(2,128)(2,1)S(1)} all-to-all(bf16[2,1024,128]{2,0,1:T(2,128)(2,1)S(1)} %copy.188), channel_id=1, replica_groups=mesh['segment'=4,'blk'=32] {'blk'}, dimensions={1} | all-to-all | bytes 1048576 | tf_op jit(solution)/shard_map/while/body/eval_jaxpr/all_to_all | solution.py:34
  224.1 365.4 %while.45 = (s32[]{:T(128)}, bf16[2,256,128]{1,2,0:T(8,128)(2,1)}, bf16[2,256,256]{1,2,0:T(8,128)(2,1)}, f32[2,256,256]{2,1,0:T(8,128)}, f32[2,64,4,1024]{3,1,2,...) while((s32[]{:T(128)}, bf16[2,256,128]{1,2,0:T(8,128)(2,1)}, ...), condition=%wide.region_3.4_spmd.clone, body=%wide.region_2.3_spmd.clone.sunk | while | flops 2403663872 | bytes 71172800 | solution.py:151
  225.0 4.8 all-to-all-start.2
  237.6 4.6 all-to-all-start.3
  265.4 5.9 select_add_fusion.7
  273.2 5.6 all-to-all-start.5
  285.0 5.4 all-to-all-done.5
  295.3 5.0 all-to-all-start.2
  308.0 4.6 all-to-all-start.3
  335.8 8.4 %select_add_fusion.7 = f32[2,1024,1024]{2,1,0:T(8,128)} fusion(f32[2,1024,1024]{2,1,0:T(8,128)} %get-tuple-element.996, f32[]{:T(128)S(6)} %convert_element_type.334, pred[]{:T(512)S(6)} %compare.3, bf16[2,1024,128]{2,1,0:T(8,128)(2,1)} %bitcast.249, f32[2,1024,128]{1,2,0:T(8,128)S(1)} %fusion.132), kind=kOutput, calls=%fused_computation.33.clone.1 | convolution fusion | flops 545521664 | bytes 18350084 | tf_op jit(solution)/shard_map/while/body/eval_jaxpr/gmt,gnt->gmn/dot_general | solution.py:59
  344.2 7.5 %all-to-all-start.5 = ((bf16[2,1024,128]{2,0,1:T(2,128)(2,1)}), bf16[2,1024,128]{2,0,1:T(2,128)(2,1)S(1)}, u32[]{:S(2)}, u32[]{:S(2)}) async-start(bf16[2,1024,128]{2,0,1:T(2,128)(2,1)} %copy.201), calls=%async_computation.5 | async-start | bytes 1048576 | tf_op jit(solution)/shard_map/while/body/eval_jaxpr/all_to_all | solution.py:34
  358.5 4.7 all-to-all-done.5
  409.4 8.4 %select_add_fusion.7 = f32[2,1024,1024]{2,1,0:T(8,128)} fusion(f32[2,1024,1024]{2,1,0:T(8,128)} %get-tuple-element.996, f32[]{:T(128)S(6)} %convert_element_type.334, pred[]{:T(512)S(6)} %compare.3, bf16[2,1024,128]{2,1,0:T(8,128)(2,1)} %bitcast.249, f32[2,1024,128]{1,2,0:T(8,128)S(1)} %fusion.132), kind=kOutput, calls=%fused_computation.33.clone.1 | convolution fusion | flops 545521664 | bytes 18350084 | tf_op jit(solution)/shard_map/while/body/eval_jaxpr/gmt,gnt->gmn/dot_general | solution.py:59
  417.7 7.5 %all-to-all-start.5 = ((bf16[2,1024,128]{2,0,1:T(2,128)(2,1)}), bf16[2,1024,128]{2,0,1:T(2,128)(2,1)S(1)}, u32[]{:S(2)}, u32[]{:S(2)}) async-start(bf16[2,1024,128]{2,0,1:T(2,128)(2,1)} %copy.201), calls=%async_computation.5 | async-start | bytes 1048576 | tf_op jit(solution)/shard_map/while/body/eval_jaxpr/all_to_all | solution.py:34
  432.1 4.7 all-to-all-done.5
  482.9 8.4 %select_add_fusion.7 = f32[2,1024,1024]{2,1,0:T(8,128)} fusion(f32[2,1024,1024]{2,1,0:T(8,128)} %get-tuple-element.996, f32[]{:T(128)S(6)} %convert_element_type.334, pred[]{:T(512)S(6)} %compare.3, bf16[2,1024,128]{2,1,0:T(8,128)(2,1)} %bitcast.249, f32[2,1024,128]{1,2,0:T(8,128)S(1)} %fusion.132), kind=kOutput, calls=%fused_computation.33.clone.1 | convolution fusion | flops 545521664 | bytes 18350084 | tf_op jit(solution)/shard_map/while/body/eval_jaxpr/gmt,gnt->gmn/dot_general | solution.py:59
  491.3 7.5 %all-to-all-start.5 = ((bf16[2,1024,128]{2,0,1:T(2,128)(2,1)}), bf16[2,1024,128]{2,0,1:T(2,128)(2,1)S(1)}, u32[]{:S(2)}, u32[]{:S(2)}) async-start(bf16[2,1024,128]{2,0,1:T(2,128)(2,1)} %copy.201), calls=%async_computation.5 | async-start | bytes 1048576 | tf_op jit(solution)/shard_map/while/body/eval_jaxpr/all_to_all | solution.py:34
  505.7 4.7 all-to-all-done.5
  556.5 8.4 %select_add_fusion.7 = f32[2,1024,1024]{2,1,0:T(8,128)} fusion(f32[2,1024,1024]{2,1,0:T(8,128)} %get-tuple-element.996, f32[]{:T(128)S(6)} %convert_element_type.334, pred[]{:T(512)S(6)} %compare.3, bf16[2,1024,128]{2,1,0:T(8,128)(2,1)} %bitcast.249, f32[2,1024,128]{1,2,0:T(8,128)S(1)} %fusion.132), kind=kOutput, calls=%fused_computation.33.clone.1 | convolution fusion | flops 545521664 | bytes 18350084 | tf_op jit(solution)/shard_map/while/body/eval_jaxpr/gmt,gnt->gmn/dot_general | solution.py:59
  564.9 7.5 %all-to-all-start.5 = ((bf16[2,1024,128]{2,0,1:T(2,128)(2,1)}), bf16[2,1024,128]{2,0,1:T(2,128)(2,1)S(1)}, u32[]{:S(2)}, u32[]{:S(2)}) async-start(bf16[2,1024,128]{2,0,1:T(2,128)(2,1)} %copy.201), calls=%async_computation.5 | async-start | bytes 1048576 | tf_op jit(solution)/shard_map/while/body/eval_jaxpr/all_to_all | solution.py:34
  579.2 4.7 all-to-all-done.5
  589.5 6.2 %convert_bitcast_fusion = bf16[1,2,1024,1024]{3,2,1,0:T(8,128)(2,1)} fusion(f32[2,1024,1024]{2,1,0:T(8,128)} %get-tuple-element.567), kind=kLoop, calls=%fused_computation.78 | loop fusion | flops 2097152 | bytes 12582912 | tf_op jit(solution)/shard_map/broadcast_in_dim | solution.py:162
  (319 shorter events, 333.8 us)
Async XLA Ops:
  48.1 6.0 collective-permute-start
  89.4 6.5 %collective-permute-start = (bf16[2,256,128]{1,2,0:T(8,128)(2,1)S(1)}, bf16[2,256,128]{1,2,0:T(8,128)(2,1)S(1)}, u32[]{:S(2)}, u32[]{:S(2)}) collective-permute-start(bf16[2,256,128]{1,2,0:T(8,128)(2,1)S(1)} %get-tuple-element.903), channel_id=1, source_target_pairs={{0,32},{32,64},{64,96},{1,33},{33,65},{65,97},{2,34},{34,66},{66,9... | collective-permute-start | bytes 393224 | tf_op jit(solution)/shard_map/while/body/eval_jaxpr/ppermute | solution.py:12
  131.3 6.5 %collective-permute-start = (bf16[2,256,128]{1,2,0:T(8,128)(2,1)S(1)}, bf16[2,256,128]{1,2,0:T(8,128)(2,1)S(1)}, u32[]{:S(2)}, u32[]{:S(2)}) collective-permute-start(bf16[2,256,128]{1,2,0:T(8,128)(2,1)S(1)} %get-tuple-element.903), channel_id=1, source_target_pairs={{0,32},{32,64},{64,96},{1,33},{33,65},{65,97},{2,34},{34,66},{66,9... | collective-permute-start | bytes 393224 | tf_op jit(solution)/shard_map/while/body/eval_jaxpr/ppermute | solution.py:12
  173.2 6.5 %collective-permute-start = (bf16[2,256,128]{1,2,0:T(8,128)(2,1)S(1)}, bf16[2,256,128]{1,2,0:T(8,128)(2,1)S(1)}, u32[]{:S(2)}, u32[]{:S(2)}) collective-permute-start(bf16[2,256,128]{1,2,0:T(8,128)(2,1)S(1)} %get-tuple-element.903), channel_id=1, source_target_pairs={{0,32},{32,64},{64,96},{1,33},{33,65},{65,97},{2,34},{34,66},{66,9... | collective-permute-start | bytes 393224 | tf_op jit(solution)/shard_map/while/body/eval_jaxpr/ppermute | solution.py:12
  215.0 6.5 %collective-permute-start = (bf16[2,256,128]{1,2,0:T(8,128)(2,1)S(1)}, bf16[2,256,128]{1,2,0:T(8,128)(2,1)S(1)}, u32[]{:S(2)}, u32[]{:S(2)}) collective-permute-start(bf16[2,256,128]{1,2,0:T(8,128)(2,1)S(1)} %get-tuple-element.903), channel_id=1, source_target_pairs={{0,32},{32,64},{64,96},{1,33},{33,65},{65,97},{2,34},{34,66},{66,9... | collective-permute-start | bytes 393224 | tf_op jit(solution)/shard_map/while/body/eval_jaxpr/ppermute | solution.py:12
  224.1 18.3 %copy-start.6 = (bf16[2,256,256]{1,2,0:T(8,128)(2,1)}, bf16[2,256,256]{1,2,0:T(8,128)(2,1)S(1)}, u32[]{:S(2)}) copy-start(bf16[2,256,256]{1,2,0:T(8,128)(2,1)S(1)} %get-tuple-element.1023) | copy-start | bytes 786436 | tf_op jit(solution)/shard_map/while
  225.0 12.5 %all-to-all-start.2 = ((bf16[2,256,128]{2,0,1:T(2,128)(2,1)}), bf16[2,256,128]{2,0,1:T(2,128)(2,1)S(1)}, u32[]{:S(2)}, u32[]{:S(2)}) async-start(bf16[2,256,128]{2,0,1:T(2,128)(2,1)} %copy.194), calls=%async_computation.2 | async-start | bytes 262144 | tf_op jit(solution)/shard_map/while/body/eval_jaxpr/all_to_all | solution.py:23
  237.6 16.3 %all-to-all-start.3 = ((bf16[64,32,128]{2,1,0:T(8,128)(2,1)}), bf16[64,32,128]{2,1,0:T(8,128)(2,1)}, u32[]{:S(2)}, u32[]{:S(2)}) async-start(bf16[64,32,128]{2,1,0:T(8,128)(2,1)} %copy.198), calls=%async_computation.3 | async-start | bytes 1048576 | tf_op jit(solution)/shard_map/while/body/eval_jaxpr/all_to_all | solution.py:58
  260.8 12.4 %all-to-all-start.4 = ((bf16[64,8,128]{2,1,0:T(8,128)(2,1)}), bf16[64,8,128]{2,1,0:T(8,128)(2,1)}, u32[]{:S(2)}, u32[]{:S(2)}) async-start(bf16[64,8,128]{2,1,0:T(8,128)(2,1)} %copy.200), calls=%async_computation.4 | async-start | bytes 262144 | tf_op jit(solution)/shard_map/while/body/eval_jaxpr/all_to_all | solution.py:73
  273.2 17.1 %all-to-all-start.5 = ((bf16[2,1024,128]{2,0,1:T(2,128)(2,1)}), bf16[2,1024,128]{2,0,1:T(2,128)(2,1)S(1)}, u32[]{:S(2)}, u32[]{:S(2)}) async-start(bf16[2,1024,128]{2,0,1:T(2,128)(2,1)} %copy.201), calls=%async_computation.5 | async-start | bytes 1048576 | tf_op jit(solution)/shard_map/while/body/eval_jaxpr/all_to_all | solution.py:34
  283.7 9.9 %collective-permute-start.1 = (bf16[2,256,128]{1,2,0:T(8,128)(2,1)S(1)}, bf16[2,256,128]{1,2,0:T(8,128)(2,1)}, u32[]{:S(2)}, u32[]{:S(2)}) collective-permute-start(bf16[2,256,128]{1,2,0:T(8,128)(2,1)S(1)} %get-tuple-element.921), channel_id=1, source_target_pairs={{32,0},{64,32},{96,64},{33,1},{65,33},{97,65},{34,2},{66,34},{98,6... | collective-permute-start | bytes 393224 | tf_op jit(solution)/shard_map/while/body/eval_jaxpr/ppermute | solution.py:12
  294.3 18.4 %copy-start.6 = (bf16[2,256,256]{1,2,0:T(8,128)(2,1)}, bf16[2,256,256]{1,2,0:T(8,128)(2,1)S(1)}, u32[]{:S(2)}) copy-start(bf16[2,256,256]{1,2,0:T(8,128)(2,1)S(1)} %get-tuple-element.1023) | copy-start | bytes 786436 | tf_op jit(solution)/shard_map/while
  295.3 12.6 %all-to-all-start.2 = ((bf16[2,256,128]{2,0,1:T(2,128)(2,1)}), bf16[2,256,128]{2,0,1:T(2,128)(2,1)S(1)}, u32[]{:S(2)}, u32[]{:S(2)}) async-start(bf16[2,256,128]{2,0,1:T(2,128)(2,1)} %copy.194), calls=%async_computation.2 | async-start | bytes 262144 | tf_op jit(solution)/shard_map/while/body/eval_jaxpr/all_to_all | solution.py:23
  308.0 16.3 %all-to-all-start.3 = ((bf16[64,32,128]{2,1,0:T(8,128)(2,1)}), bf16[64,32,128]{2,1,0:T(8,128)(2,1)}, u32[]{:S(2)}, u32[]{:S(2)}) async-start(bf16[64,32,128]{2,1,0:T(8,128)(2,1)} %copy.198), calls=%async_computation.3 | async-start | bytes 1048576 | tf_op jit(solution)/shard_map/while/body/eval_jaxpr/all_to_all | solution.py:58
  331.2 13.0 %all-to-all-start.4 = ((bf16[64,8,128]{2,1,0:T(8,128)(2,1)}), bf16[64,8,128]{2,1,0:T(8,128)(2,1)}, u32[]{:S(2)}, u32[]{:S(2)}) async-start(bf16[64,8,128]{2,1,0:T(8,128)(2,1)} %copy.200), calls=%async_computation.4 | async-start | bytes 262144 | tf_op jit(solution)/shard_map/while/body/eval_jaxpr/all_to_all | solution.py:73
  344.2 19.0 %all-to-all-start.5 = ((bf16[2,1024,128]{2,0,1:T(2,128)(2,1)}), bf16[2,1024,128]{2,0,1:T(2,128)(2,1)S(1)}, u32[]{:S(2)}, u32[]{:S(2)}) async-start(bf16[2,1024,128]{2,0,1:T(2,128)(2,1)} %copy.201), calls=%async_computation.5 | async-start | bytes 1048576 | tf_op jit(solution)/shard_map/while/body/eval_jaxpr/all_to_all | solution.py:34
  357.3 10.8 %collective-permute-start.1 = (bf16[2,256,128]{1,2,0:T(8,128)(2,1)S(1)}, bf16[2,256,128]{1,2,0:T(8,128)(2,1)}, u32[]{:S(2)}, u32[]{:S(2)}) collective-permute-start(bf16[2,256,128]{1,2,0:T(8,128)(2,1)S(1)} %get-tuple-element.921), channel_id=1, source_target_pairs={{32,0},{64,32},{96,64},{33,1},{65,33},{97,65},{34,2},{66,34},{98,6... | collective-permute-start | bytes 393224 | tf_op jit(solution)/shard_map/while/body/eval_jaxpr/ppermute | solution.py:12
  369.8 11.7 %all-to-all-start.2 = ((bf16[2,256,128]{2,0,1:T(2,128)(2,1)}), bf16[2,256,128]{2,0,1:T(2,128)(2,1)S(1)}, u32[]{:S(2)}, u32[]{:S(2)}) async-start(bf16[2,256,128]{2,0,1:T(2,128)(2,1)} %copy.194), calls=%async_computation.2 | async-start | bytes 262144 | tf_op jit(solution)/shard_map/while/body/eval_jaxpr/all_to_all | solution.py:23
  381.5 16.3 %all-to-all-start.3 = ((bf16[64,32,128]{2,1,0:T(8,128)(2,1)}), bf16[64,32,128]{2,1,0:T(8,128)(2,1)}, u32[]{:S(2)}, u32[]{:S(2)}) async-start(bf16[64,32,128]{2,1,0:T(8,128)(2,1)} %copy.198), calls=%async_computation.3 | async-start | bytes 1048576 | tf_op jit(solution)/shard_map/while/body/eval_jaxpr/all_to_all | solution.py:58
  404.7 13.0 %all-to-all-start.4 = ((bf16[64,8,128]{2,1,0:T(8,128)(2,1)}), bf16[64,8,128]{2,1,0:T(8,128)(2,1)}, u32[]{:S(2)}, u32[]{:S(2)}) async-start(bf16[64,8,128]{2,1,0:T(8,128)(2,1)} %copy.200), calls=%async_computation.4 | async-start | bytes 262144 | tf_op jit(solution)/shard_map/while/body/eval_jaxpr/all_to_all | solution.py:73
  417.7 19.1 %all-to-all-start.5 = ((bf16[2,1024,128]{2,0,1:T(2,128)(2,1)}), bf16[2,1024,128]{2,0,1:T(2,128)(2,1)S(1)}, u32[]{:S(2)}, u32[]{:S(2)}) async-start(bf16[2,1024,128]{2,0,1:T(2,128)(2,1)} %copy.201), calls=%async_computation.5 | async-start | bytes 1048576 | tf_op jit(solution)/shard_map/while/body/eval_jaxpr/all_to_all | solution.py:34
  430.8 10.8 %collective-permute-start.1 = (bf16[2,256,128]{1,2,0:T(8,128)(2,1)S(1)}, bf16[2,256,128]{1,2,0:T(8,128)(2,1)}, u32[]{:S(2)}, u32[]{:S(2)}) collective-permute-start(bf16[2,256,128]{1,2,0:T(8,128)(2,1)S(1)} %get-tuple-element.921), channel_id=1, source_target_pairs={{32,0},{64,32},{96,64},{33,1},{65,33},{97,65},{34,2},{66,34},{98,6... | collective-permute-start | bytes 393224 | tf_op jit(solution)/shard_map/while/body/eval_jaxpr/ppermute | solution.py:12
  443.4 11.7 %all-to-all-start.2 = ((bf16[2,256,128]{2,0,1:T(2,128)(2,1)}), bf16[2,256,128]{2,0,1:T(2,128)(2,1)S(1)}, u32[]{:S(2)}, u32[]{:S(2)}) async-start(bf16[2,256,128]{2,0,1:T(2,128)(2,1)} %copy.194), calls=%async_computation.2 | async-start | bytes 262144 | tf_op jit(solution)/shard_map/while/body/eval_jaxpr/all_to_all | solution.py:23
  455.1 16.3 %all-to-all-start.3 = ((bf16[64,32,128]{2,1,0:T(8,128)(2,1)}), bf16[64,32,128]{2,1,0:T(8,128)(2,1)}, u32[]{:S(2)}, u32[]{:S(2)}) async-start(bf16[64,32,128]{2,1,0:T(8,128)(2,1)} %copy.198), calls=%async_computation.3 | async-start | bytes 1048576 | tf_op jit(solution)/shard_map/while/body/eval_jaxpr/all_to_all | solution.py:58
  478.3 13.0 %all-to-all-start.4 = ((bf16[64,8,128]{2,1,0:T(8,128)(2,1)}), bf16[64,8,128]{2,1,0:T(8,128)(2,1)}, u32[]{:S(2)}, u32[]{:S(2)}) async-start(bf16[64,8,128]{2,1,0:T(8,128)(2,1)} %copy.200), calls=%async_computation.4 | async-start | bytes 262144 | tf_op jit(solution)/shard_map/while/body/eval_jaxpr/all_to_all | solution.py:73
  491.3 19.1 %all-to-all-start.5 = ((bf16[2,1024,128]{2,0,1:T(2,128)(2,1)}), bf16[2,1024,128]{2,0,1:T(2,128)(2,1)S(1)}, u32[]{:S(2)}, u32[]{:S(2)}) async-start(bf16[2,1024,128]{2,0,1:T(2,128)(2,1)} %copy.201), calls=%async_computation.5 | async-start | bytes 1048576 | tf_op jit(solution)/shard_map/while/body/eval_jaxpr/all_to_all | solution.py:34
  504.4 10.8 %collective-permute-start.1 = (bf16[2,256,128]{1,2,0:T(8,128)(2,1)S(1)}, bf16[2,256,128]{1,2,0:T(8,128)(2,1)}, u32[]{:S(2)}, u32[]{:S(2)}) collective-permute-start(bf16[2,256,128]{1,2,0:T(8,128)(2,1)S(1)} %get-tuple-element.921), channel_id=1, source_target_pairs={{32,0},{64,32},{96,64},{33,1},{65,33},{97,65},{34,2},{66,34},{98,6... | collective-permute-start | bytes 393224 | tf_op jit(solution)/shard_map/while/body/eval_jaxpr/ppermute | solution.py:12
  516.9 11.7 %all-to-all-start.2 = ((bf16[2,256,128]{2,0,1:T(2,128)(2,1)}), bf16[2,256,128]{2,0,1:T(2,128)(2,1)S(1)}, u32[]{:S(2)}, u32[]{:S(2)}) async-start(bf16[2,256,128]{2,0,1:T(2,128)(2,1)} %copy.194), calls=%async_computation.2 | async-start | bytes 262144 | tf_op jit(solution)/shard_map/while/body/eval_jaxpr/all_to_all | solution.py:23
  528.6 16.3 %all-to-all-start.3 = ((bf16[64,32,128]{2,1,0:T(8,128)(2,1)}), bf16[64,32,128]{2,1,0:T(8,128)(2,1)}, u32[]{:S(2)}, u32[]{:S(2)}) async-start(bf16[64,32,128]{2,1,0:T(8,128)(2,1)} %copy.198), calls=%async_computation.3 | async-start | bytes 1048576 | tf_op jit(solution)/shard_map/while/body/eval_jaxpr/all_to_all | solution.py:58
  551.9 13.0 %all-to-all-start.4 = ((bf16[64,8,128]{2,1,0:T(8,128)(2,1)}), bf16[64,8,128]{2,1,0:T(8,128)(2,1)}, u32[]{:S(2)}, u32[]{:S(2)}) async-start(bf16[64,8,128]{2,1,0:T(8,128)(2,1)} %copy.200), calls=%async_computation.4 | async-start | bytes 262144 | tf_op jit(solution)/shard_map/while/body/eval_jaxpr/all_to_all | solution.py:73
  564.9 19.1 %all-to-all-start.5 = ((bf16[2,1024,128]{2,0,1:T(2,128)(2,1)}), bf16[2,1024,128]{2,0,1:T(2,128)(2,1)S(1)}, u32[]{:S(2)}, u32[]{:S(2)}) async-start(bf16[2,1024,128]{2,0,1:T(2,128)(2,1)} %copy.201), calls=%async_computation.5 | async-start | bytes 1048576 | tf_op jit(solution)/shard_map/while/body/eval_jaxpr/all_to_all | solution.py:34
  577.9 10.8 %collective-permute-start.1 = (bf16[2,256,128]{1,2,0:T(8,128)(2,1)S(1)}, bf16[2,256,128]{1,2,0:T(8,128)(2,1)}, u32[]{:S(2)}, u32[]{:S(2)}) collective-permute-start(bf16[2,256,128]{1,2,0:T(8,128)(2,1)S(1)} %get-tuple-element.921), channel_id=1, source_target_pairs={{32,0},{64,32},{96,64},{33,1},{65,33},{97,65},{34,2},{66,34},{98,6... | collective-permute-start | bytes 393224 | tf_op jit(solution)/shard_map/while/body/eval_jaxpr/ppermute | solution.py:12
  (38 other events, 189.1 us)
where the time goes:
time: 605 us; the launch traced here: 601 us
  matrix products  160 us (26%)
  blocking collectives  140 us (23%)
  starting transfers between devices  130 us (21%)
  waiting for transfers between devices  81.4 us (13%)
  local copies, waits for them, and re-layouts  74.1 us (12%)
  other arithmetic  13.1 us (2%)
    all_to_all x5, blocking collectives, forward_layer(): lax.all_to_all(spread, 'blk', split_axis=1, concat_axis=0, tiled=True)  76 us
    all_to_all x5, blocking collectives, forward_layer(): lax.all_to_all(mixed, 'blk', split_axis=1, concat_axis=0, tiled=True)  64.4 us
    dot_general x10, matrix products, forward_layer(): jnp.einsum('gmt,gmn->gnt', activated, third, preferred_element_type=jnp.f...  40.6 us
    dot_general x5, matrix products, backward_layer(): jnp.einsum('gmt,gnt->gmn', activated, grad_spread, preferred_element_type...  39.4 us
    all_to_all x5, starting transfers between devices, forward_layer(): lax.all_to_all(spread, 'blk', split_axis=1, concat_axis=0, tiled=True)  35.5 us
    ppermute x10, starting transfers between devices, shifted(): return lax.ppermute(block, axis, route)  26.4 us
    all_to_all x5, waiting for transfers between devices, forward_layer(): lax.all_to_all(spread, 'blk', split_axis=1, concat_axis=0, tiled=True)  24.2 us
    all_to_all x5, starting transfers between devices, backward_layer(): lax.all_to_all(back_spread, 'blk', split_axis=0, concat_axis=1, tiled=True)  23 us
  transfers between devices with their start and end apart: 30, of which 21 were waited for; matrix products, arithmetic and copies ran while one was open for 23% of the time, Pallas kernels for 0%

commit v1 on v0

v1 whole, which is shorter than its diff:
```python
import functools

import jax
import jax.numpy as jnp
from jax import lax
from jax.experimental import pallas as pl
from jax.experimental.pallas import tpu as pltpu
from jax.sharding import PartitionSpec as P

CHAINS = 1
VMEM_BYTES = 24 * 1024 * 1024
BF16 = jnp.bfloat16
F32 = jnp.float32
CUBIC = 0.044715
ROOT = 0.7978845608028654


def call(body, outs, *args):
    place = pl.BlockSpec(memory_space=pltpu.VMEM)
    scalar = pl.BlockSpec(memory_space=pltpu.SMEM)
    specs = [scalar if arg.dtype == jnp.int32 else place for arg in args]
    return pl.pallas_call(
        body,
        out_shape=[jax.ShapeDtypeStruct(shape, BF16) for shape in outs],
        in_specs=specs,
        out_specs=[place] * len(outs),
        compiler_params=pltpu.CompilerParams(vmem_limit_bytes=VMEM_BYTES),
    )(*args)


def dot(left, right):
    return lax.dot_general(left, right, (((1,), (0,)), ((), ())), preferred_element_type=F32)


def dot_nt(left, right):
    return lax.dot_general(left, right, (((1,), (1,)), ((), ())), preferred_element_type=F32)


def spots(rows, columns, row_key, column_key):
    row = lax.broadcasted_iota(jnp.int32, (rows, columns), 0)
    column = lax.broadcasted_iota(jnp.int32, (rows, columns), 1)
    return jnp.where(row_key(row) == column_key(column), 1.0, 0.0).astype(BF16)


def picks_first(k, inner):
    rows, columns = 512, 256

    def row_key(r):
        inside = r % (2 * inner)
        return jnp.where(inside // inner == k, (r // (2 * inner)) * inner + inside % inner, -1)

    return spots(rows, columns, row_key, lambda c: c)


def picks_second(g, inner):
    rows, columns = 512, 256
    half = 2 * inner

    def row_key(r):
        inside = r % (2 * half)
        return jnp.where(inside // half == g, (r // (2 * half)) * half + inside % half, -1)

    return spots(rows, columns, row_key, lambda c: c)


def prepare_first(w1, up, down):
    for k in range(2):
        pick = picks_first(k, 4)
        up[:, 256 * k : 256 * (k + 1)] = dot_nt(pick, w1[k]).astype(BF16)
        down[256 * k : 256 * (k + 1), :] = dot_nt(w1[k], pick).astype(BF16)


def prepare_second(w2, up, down):
    for g in range(2):
        pick = picks_second(g, 4)
        wide = dot(pick, w2[g]).astype(BF16)
        down[:, 1024 * g : 1024 * (g + 1)] = wide
        up[1024 * g : 1024 * (g + 1), :] = wide.T


def enter(x, w1_up, mixed):
    mixed[...] = dot(w1_up[...], x[...]).astype(BF16).reshape(mixed.shape)


def enter_choice(choose, arrived, x, w1_up, x_now, mixed):
    now = jnp.where(choose[0] > 0, arrived[...], x[...])
    x_now[...] = now
    mixed[...] = dot(w1_up[...], now).astype(BF16).reshape(mixed.shape)


def gelu_tanh(value):
    return jnp.tanh(ROOT * (value + CUBIC * (value * value * value)))


def middle(arrived, w2_up, w3_up, spread, *kept):
    joined = arrived[...].reshape(512, arrived.shape[2])
    for g in range(2):
        pre = dot(w2_up[1024 * g : 1024 * (g + 1), :], joined).astype(BF16)
        wide = pre.astype(F32)
        activated = (0.5 * wide * (1.0 + gelu_tanh(wide))).astype(BF16)
        if kept:
            kept[0][g] = pre
            kept[1][g] = activated
        out = dot(w3_up[g], activated).astype(BF16)
        spread[:, 32 * g : 32 * (g + 1), :] = out.reshape(32, 32, out.shape[1])


def leave(arrived, w4_up, x, out):
    for k in range(2):
        rows = slice(256 * k, 256 * (k + 1))
        part = arrived[...].reshape(64, 32, arrived.shape[2])[:, 16 * k : 16 * (k + 1), :]
        total = dot(w4_up[k], part.reshape(1024, part.shape[2]))
        out[rows, :] = (x[rows, :].astype(F32) + total).astype(BF16)


def back_enter_from(now, w4, spread):
    parts = []
    for k in range(2):
        part = dot(w4[k], now[256 * k : 256 * (k + 1), :]).astype(BF16)
        parts.append(part.reshape(64, 1, 16, part.shape[1]))
    joined = jnp.concatenate(parts, axis=1)
    spread[...] = joined.reshape(spread.shape)


def back_enter(upstream, w4, spread):
    back_enter_from(upstream[...], w4, spread)


def back_enter_choice(choose, arrived, upstream, w4, now_out, spread):
    now = jnp.where(choose[0] > 0, arrived[...], upstream[...])
    now_out[...] = now
    back_enter_from(now, w4, spread)


def back_middle(arrived, w3, w2_down, pre, back, *kept):
    total = None
    for g in range(2):
        part = arrived[:, 32 * g : 32 * (g + 1), :]
        part = part.reshape(1024, part.shape[2])
        grad = dot(w3[g], part)
        value = pre[g].astype(F32)
        bend = gelu_tanh(value)
        slope = ROOT * (1.0 + 3.0 * CUBIC * (value * value))
        factor = 0.5 * (1.0 + bend) + (0.5 * value * (1.0 - bend * bend)) * slope
        grad_pre = (grad * factor).astype(BF16)
        if kept:
            kept[0][g] = grad_pre
        term = dot(w2_down[:, 1024 * g : 1024 * (g + 1)], grad_pre)
        total = term if total is None else total + term
    back[...] = total.astype(BF16).reshape(back.shape)


def back_leave(arrived, w1_down, upstream, out):
    total = dot(w1_down[...], arrived[...].reshape(512, arrived.shape[2]))
    out[...] = (upstream[...].astype(F32) + total).astype(BF16)


def grads_fourth(arrived, up, grad):
    for k in range(2):
        part = arrived[...].reshape(64, 32, arrived.shape[2])[:, 16 * k : 16 * (k + 1), :]
        part = part.reshape(1024, part.shape[2])
        grad[k] = dot_nt(part, up[256 * k : 256 * (k + 1), :]).astype(BF16)


def grads_third(act, back, grad):
    for g in range(2):
        part = back[:, 32 * g : 32 * (g + 1), :]
        part = part.reshape(1024, part.shape[2])
        for start in range(0, 1024, 256):
            grad[g, start : start + 256, :] = dot_nt(act[g, start : start + 256, :], part).astype(BF16)


def grads_second(mixed, pre, grad):
    for g in range(2):
        total = dot_nt(mixed[...].reshape(512, mixed.shape[2]), pre[g])
        total = total.reshape(32, 16, 1024)[:, 8 * g : 8 * (g + 1), :]
        grad[g] = total.reshape(256, 1024).astype(BF16)


def grads_first(x, back, grad):
    for k in range(2):
        pick = picks_first(k, 4)
        term = dot_nt(x[256 * k : 256 * (k + 1), :], back[...].reshape(512, back.shape[2]))
        grad[k] = dot(term.astype(BF16), pick).astype(BF16)


def exchange(block):
    return lax.all_to_all(block, "blk", split_axis=0, concat_axis=0, tiled=True)


def shards(tokens, cotangent, first_factor, second_factor, third_factor, fourth_factor):
    segments = lax.axis_size("segment")
    position = lax.axis_index("segment")
    total = tokens.shape[0]
    part = total // CHAINS
    w1, w2, w3, w4 = first_factor[0], second_factor[0], third_factor[0], fourth_factor[0]
    w1_up, w1_down = call(prepare_first, [(512, 512), (512, 512)], w1)
    entry = tokens.T
    x = [entry[:, part * h : part * (h + 1)] for h in range(CHAINS)]
    w2_up, w2_down = call(prepare_second, [(2048, 512), (512, 2048)], w2)
    w3_up = w3.transpose(0, 2, 1)
    w4_up = w4.transpose(0, 2, 1)

    chunk = (32, 16, part)
    wide = (32, 64, part)
    flat = (512, part)
    inner = (2, 1024, part)
    mixed_in = [None] * CHAINS
    pres = [None] * CHAINS
    acts = [None] * CHAINS
    spreads = [None] * CHAINS
    outs = [None] * CHAINS
    incoming = [None] * CHAINS
    for step in range(segments):
        last = step == segments - 1
        choose = (position == step).astype(jnp.int32).reshape(1)
        for h in range(CHAINS):
            if step == 0:
                (mixed,) = call(enter, [chunk], x[h], w1_up)
            else:
                x[h], mixed = call(enter_choice, [flat, chunk], choose, incoming[h], x[h], w1_up)
            arrived = exchange(mixed)
            if last:
                mixed_in[h] = arrived
                spread, pres[h], acts[h] = call(middle, [wide, inner, inner], arrived, w2_up, w3_up)
            else:
                (spread,) = call(middle, [wide], arrived, w2_up, w3_up)
            arrived = exchange(spread)
            (outs[h],) = call(leave, [flat], arrived, w4_up, x[h])
            if last:
                spreads[h] = arrived
            else:
                incoming[h] = lax.ppermute(outs[h], "segment", [(step, step + 1)])

    returning = cotangent.T
    up = [returning[:, part * h : part * (h + 1)] for h in range(CHAINS)]
    back_spread = [None] * CHAINS
    grad_pres = [None] * CHAINS
    back_mixed = [None] * CHAINS
    grads = [None] * CHAINS
    for step in range(segments):
        last = step == segments - 1
        choose = (position == segments - 1 - step).astype(jnp.int32).reshape(1)
        for h in range(CHAINS):
            if step == 0:
                (spread,) = call(back_enter, [wide], up[h], w4)
            else:
                up[h], spread = call(back_enter_choice, [flat, wide], choose, incoming[h], up[h], w4)
            back_spread[h] = exchange(spread)
            if last:
                back, grad_pres[h] = call(
                    back_middle, [chunk, inner], back_spread[h], w3, w2_down, pres[h]
                )
            else:
                (back,) = call(back_middle, [chunk], back_spread[h], w3, w2_down, pres[h])
            back_mixed[h] = exchange(back)
            (grads[h],) = call(back_leave, [flat], back_mixed[h], w1_down, up[h])
            if not last:
                source = segments - 1 - step
                incoming[h] = lax.ppermute(grads[h], "segment", [(source, source - 1)])

    (fourth_grad,) = call(grads_fourth, [w4.shape], *spreads, *up)
    (third_grad,) = call(grads_third, [w3.shape], *acts, *back_spread)
    (second_grad,) = call(grads_second, [w2.shape], *mixed_in, *grad_pres)
    (first_grad,) = call(grads_first, [w1.shape], *x, *back_mixed)
    segment_outputs = jnp.concatenate([out.T for out in outs], axis=0)
    input_grads = jnp.concatenate([grad.T for grad in grads], axis=0)
    return (
        segment_outputs[None],
        input_grads[None],
        first_grad[None],
        second_grad[None],
        third_grad[None],
        fourth_grad[None],
    )


def solution(mesh):
    placed = (
        P(None, "blk"),
        P(None, "blk"),
        P("segment", "blk", None, None),
        P("segment", "blk", None, None),
        P("segment", "blk", None, None),
        P("segment", "blk", None, None),
    )
    return jax.shard_map(
        shards,
        mesh=mesh,
        in_specs=placed,
        out_specs=(
            P("segment", None, "blk"),
            P("segment", None, "blk"),
            P("segment", "blk", None, None),
            P("segment", "blk", None, None),
            P("segment", "blk", None, None),
            P("segment", "blk", None, None),
        ),
        check_vma=False,
    )
```

time: 605 us -> 401 us (0.66)
  matrix products: 160 us -> 0 us
  starting transfers between devices: 130 us -> 43.5 us
  Pallas kernels: 0 us -> 50.9 us
  blocking collectives: 140 us -> 168 us
  local copies, waits for them, and re-layouts: 74.1 us -> 51 us
  other arithmetic: 13.1 us -> 0 us
    dot_general x70 -> x0, matrix products: 160 us -> none  [the longest x10 40.6 us: forward_layer(): jnp.einsum('gmt,gmn->gnt', activated, third, preferred_element_type=jnp.f...]
    all_to_all x20 -> x6, starting transfers between devices: 103 us -> 33.8 us  [exchange(): return lax.all_to_all(block, 'blk', split_axis=0, concat_axis=0, tiled=True)]
    pallas_call x0 -> x30, Pallas kernels: none -> 50.9 us  [call(): pl.pallas_call(body, out_shape=[jax.ShapeDtypeStruct(shape, BF16) for sha...]
    unnamed x13 -> x94, local copies, waits for them, and re-layouts: 5.95 us -> 43.5 us
    ppermute x10 -> x6, waiting for transfers between devices: 12 us -> 45.6 us  [the longest x3 40.7 us: shards(): incoming[h] = lax.ppermute(grads[h], 'segment', [(source, source - 1)])]
    all_to_all x20 -> x6, waiting for transfers between devices: 69.4 us -> 39.3 us  [exchange(): return lax.all_to_all(block, 'blk', split_axis=0, concat_axis=0, tiled=True)]
    all_to_all x10, blocking collectives: 140 us -> 168 us  [exchange(): return lax.all_to_all(block, 'blk', split_axis=0, concat_axis=0, tiled=True)]
    convert_element_type x22 -> x0, local copies, waits for them, and re-layouts: 23 us -> none  [the longest x10 16.6 us: forward_layer(): spread = jnp.einsum('gmt,gmn->gnt', activated, third, preferred_element_t...]
  transfers between devices with their start and end apart: 30 -> 12, of which waited for: 21 -> 6; matrix products, arithmetic and copies ran while one was open for 23% -> 2% of each run, Pallas kernels for 0% -> 5%
where the time goes in v1:
time: 401 us; the launch traced here: 399 us
  blocking collectives  168 us (42%)
  waiting for transfers between devices  84.8 us (21%)
  local copies, waits for them, and re-layouts  51 us (13%)
  Pallas kernels  50.9 us (13%)
  starting transfers between devices  43.5 us (11%)
    all_to_all x10, blocking collectives, exchange(): return lax.all_to_all(block, 'blk', split_axis=0, concat_axis=0, tiled=True)  168 us
    pallas_call x30, Pallas kernels, call(): pl.pallas_call(body, out_shape=[jax.ShapeDtypeStruct(shape, BF16) for sha...  50.9 us
    unnamed x94, local copies, waits for them, and re-layouts  43.5 us
    ppermute x3, waiting for transfers between devices, shards(): incoming[h] = lax.ppermute(grads[h], 'segment', [(source, source - 1)])  40.7 us
    all_to_all x6, waiting for transfers between devices, exchange(): return lax.all_to_all(block, 'blk', split_axis=0, concat_axis=0, tiled=True)  39.3 us
    all_to_all x6, starting transfers between devices, exchange(): return lax.all_to_all(block, 'blk', split_axis=0, concat_axis=0, tiled=True)  33.8 us
  transfers between devices with their start and end apart: 12, of which 6 were waited for; matrix products, arithmetic and copies ran while one was open for 2% of the time, Pallas kernels for 5%

profile of v1, /device:TPU:1, one launch (start us, length us, event | category | flops | bytes accessed | tf_op | source)
XLA Modules:
  0.0 398.9 jit_solution(5422855353298130681)
XLA Ops:
  5.8 8.6 %all-to-all-start = ((bf16[32,16,256]{2,1,0:T(8,128)(2,1)}), bf16[32,16,256]{2,1,0:T(8,128)(2,1)}, u32[]{:S(2)}, u32[]{:S(2)}) async-start(bf16[32,16,256]{2,1,0:T(8,128)(2,1)} %shard_map.110), calls=%async_computation | async-start | bytes 524288 | tf_op jit(solution)/shard_map/all_to_all | solution.py:188
  17.8 6.2 %copy.13.w3_up = bf16[2,1024,1024]{2,1,0:T(8,128)(2,1)} copy(bf16[2,1024,1024]{1,2,0:T(8,128)(2,1)} %bitcast.24) | data formatting | bytes 8388608 | tf_op jit(solution)/shard_map/transpose | solution.py:201
  26.2 3.1 shard_map.112
  30.3 7.4 %all-to-all-start.1 = ((bf16[32,64,256]{2,1,0:T(8,128)(2,1)}), bf16[32,64,256]{2,1,0:T(8,128)(2,1)}, u32[]{:S(2)}, u32[]{:S(2)}) async-start(bf16[32,64,256]{2,1,0:T(8,128)(2,1)} %copy-done.28), calls=%async_computation.1 | async-start | bytes 2097152 | tf_op jit(solution)/shard_map/all_to_all | solution.py:188
  39.0 15.9 %all-to-all-done.1.arrived = bf16[32,64,256]{2,1,0:T(8,128)(2,1)} async-done(((bf16[32,64,256]{2,1,0:T(8,128)(2,1)}), bf16[32,64,256]{2,1,0:T(8,128)(2,1)}, u32[]{:S(2)}, u32[]{:S(2)}) %all-to-all-start.1) | async-done | bytes 1048608 | tf_op jit(solution)/shard_map/all_to_all | solution.py:188
  58.5 4.3 %collective-permute-start = (bf16[512,256]{1,0:T(8,128)(2,1)}, bf16[512,256]{1,0:T(8,128)(2,1)}, u32[]{:S(2)}, u32[]{:S(2)}) collective-permute-start(bf16[512,256]{1,0:T(8,128)(2,1)} %shard_map.113), channel_id=1, source_target_pairs={{0,32},{1,33},{2,34},{3,35},{4,36},{5,37},{6,38},{7,39},{8,40},{9,... | collective-permute-start | bytes 786440 | tf_op jit(solution)/shard_map/ppermute | solution.py:233
  62.8 4.9 %collective-permute-done.arrived = bf16[512,256]{1,0:T(8,128)(2,1)} collective-permute-done((bf16[512,256]{1,0:T(8,128)(2,1)}, bf16[512,256]{1,0:T(8,128)(2,1)}, u32[]{:S(2)}, u32[]{:S(2)}) %collective-permute-start) | collective-permute-done | bytes 262176 | tf_op jit(solution)/shard_map/ppermute | solution.py:233
  70.0 13.3 %all_to_all.80.arrived = bf16[32,16,256]{2,1,0:T(8,128)(2,1)S(1)} all-to-all(bf16[32,16,256]{2,1,0:T(8,128)(2,1)S(1)} %get-tuple-element.29), channel_id=1, replica_groups=mesh['segment'=4,'blk'=32] {'blk'}, dimensions={0} | all-to-all | bytes 524288 | tf_op jit(solution)/shard_map/all_to_all | solution.py:188
  87.6 20.7 %all_to_all.81.arrived = bf16[32,64,256]{2,1,0:T(8,128)(2,1)S(1)} all-to-all(bf16[32,64,256]{2,1,0:T(8,128)(2,1)S(1)} %shard_map.115), channel_id=1, replica_groups=mesh['segment'=4,'blk'=32] {'blk'}, dimensions={0} | all-to-all | bytes 2097152 | tf_op jit(solution)/shard_map/all_to_all | solution.py:188
  113.4 12.4 %all_to_all.82.arrived = bf16[32,16,256]{2,1,0:T(8,128)(2,1)S(1)} all-to-all(bf16[32,16,256]{2,1,0:T(8,128)(2,1)S(1)} %get-tuple-element.31), channel_id=1, replica_groups=mesh['segment'=4,'blk'=32] {'blk'}, dimensions={0} | all-to-all | bytes 524288 | tf_op jit(solution)/shard_map/all_to_all | solution.py:188
  130.0 20.7 %all_to_all.83.arrived = bf16[32,64,256]{2,1,0:T(8,128)(2,1)S(1)} all-to-all(bf16[32,64,256]{2,1,0:T(8,128)(2,1)S(1)} %shard_map.118), channel_id=1, replica_groups=mesh['segment'=4,'blk'=32] {'blk'}, dimensions={0} | all-to-all | bytes 2097152 | tf_op jit(solution)/shard_map/all_to_all | solution.py:188
  157.0 4.6 %all-to-all-start.6 = ((bf16[32,16,256]{2,1,0:T(8,128)(2,1)}), bf16[32,16,256]{2,1,0:T(8,128)(2,1)}, u32[]{:S(2)}, u32[]{:S(2)}) async-start(bf16[32,16,256]{2,1,0:T(8,128)(2,1)} %copy-done.44), calls=%async_computation.6 | async-start | bytes 524288 | tf_op jit(solution)/shard_map/all_to_all | solution.py:188
  164.1 6.5 %all-to-all-done.6.arrived.mixed = bf16[32,16,256]{2,1,0:T(8,128)(2,1)} async-done(((bf16[32,16,256]{2,1,0:T(8,128)(2,1)}), bf16[32,16,256]{2,1,0:T(8,128)(2,1)}, u32[]{:S(2)}, u32[]{:S(2)}) %all-to-all-start.6) | async-done | bytes 262176 | tf_op jit(solution)/shard_map/all_to_all | solution.py:188
  170.6 4.5 %all-to-all-start.8 = ((bf16[32,64,256]{2,1,0:T(8,128)(2,1)}), bf16[32,64,256]{2,1,0:T(8,128)(2,1)}, u32[]{:S(2)}, u32[]{:S(2)}) async-start(bf16[32,64,256]{2,1,0:T(8,128)(2,1)} %copy-done.27), calls=%async_computation.8 | async-start | bytes 2097152 | tf_op jit(solution)/shard_map/all_to_all | solution.py:188
  177.3 3.1 shard_map.121
  183.3 9.1 %all-to-all-done.8.arrived = bf16[32,64,256]{2,1,0:T(8,128)(2,1)} async-done(((bf16[32,64,256]{2,1,0:T(8,128)(2,1)}), bf16[32,64,256]{2,1,0:T(8,128)(2,1)}, u32[]{:S(2)}, u32[]{:S(2)}) %all-to-all-start.8) | async-done | bytes 1048608 | tf_op jit(solution)/shard_map/all_to_all | solution.py:188
  197.5 4.5 %shard_map.124 = bf16[32,16,256]{2,1,0:T(8,128)(2,1)S(1)} custom-call(bf16[32,64,256]{2,1,0:T(8,128)(2,1)} %all-to-all-done.8.arrived, bf16[2,1024,1024]{2,1,0:T(8,128)(2,1)S(1)} %bitcast.25, bf16[512,2048]{1,0:T(8,128)(2,1)S(1)} %copy-done.8, bf16[2,1024,256]{2,1,0:T(8,128)(2,1)S(1)} %copy-done.16), custom_call_target="tpu_custom_call" | custom-call | tf_op jit(solution)/shard_map/pallas_call | solution.py:22
  202.0 12.6 %all_to_all.84.arrived = bf16[32,16,256]{2,1,0:T(8,128)(2,1)S(1)} all-to-all(bf16[32,16,256]{2,1,0:T(8,128)(2,1)S(1)} %shard_map.124), channel_id=1, replica_groups=mesh['segment'=4,'blk'=32] {'blk'}, dimensions={0} | all-to-all | bytes 524288 | tf_op jit(solution)/shard_map/all_to_all | solution.py:188
  216.1 20.7 %all_to_all.85.arrived = bf16[32,64,256]{2,1,0:T(8,128)(2,1)S(1)} all-to-all(bf16[32,64,256]{2,1,0:T(8,128)(2,1)S(1)} %get-tuple-element.39), channel_id=1, replica_groups=mesh['segment'=4,'blk'=32] {'blk'}, dimensions={0} | all-to-all | bytes 2097152 | tf_op jit(solution)/shard_map/all_to_all | solution.py:188
  236.8 3.2 shard_map.127
  240.1 12.4 %all_to_all.86.arrived = bf16[32,16,256]{2,1,0:T(8,128)(2,1)S(1)} all-to-all(bf16[32,16,256]{2,1,0:T(8,128)(2,1)S(1)} %shard_map.127), channel_id=1, replica_groups=mesh['segment'=4,'blk'=32] {'blk'}, dimensions={0} | all-to-all | bytes 524288 | tf_op jit(solution)/shard_map/all_to_all | solution.py:188
  253.9 20.7 %all_to_all.87.arrived = bf16[32,64,256]{2,1,0:T(8,128)(2,1)S(1)} all-to-all(bf16[32,64,256]{2,1,0:T(8,128)(2,1)S(1)} %get-tuple-element.41), channel_id=1, replica_groups=mesh['segment'=4,'blk'=32] {'blk'}, dimensions={0} | all-to-all | bytes 2097152 | tf_op jit(solution)/shard_map/all_to_all | solution.py:188
  274.6 3.2 shard_map.130
  277.9 12.6 %all_to_all.88.arrived = bf16[32,16,256]{2,1,0:T(8,128)(2,1)S(1)} all-to-all(bf16[32,16,256]{2,1,0:T(8,128)(2,1)S(1)} %shard_map.130), channel_id=1, replica_groups=mesh['segment'=4,'blk'=32] {'blk'}, dimensions={0} | all-to-all | bytes 524288 | tf_op jit(solution)/shard_map/all_to_all | solution.py:188
  292.8 40.7 %collective-permute-done.5.arrived = bf16[512,256]{1,0:T(8,128)(2,1)} collective-permute-done((bf16[512,256]{1,0:T(8,128)(2,1)}, bf16[512,256]{1,0:T(8,128)(2,1)}, u32[]{:S(2)}, u32[]{:S(2)}) %collective-permute-start.5) | collective-permute-done | bytes 262176 | tf_op jit(solution)/shard_map/ppermute | solution.py:260
  335.5 21.3 %all_to_all.89.arrived.back = bf16[32,64,256]{2,1,0:T(8,128)(2,1)} all-to-all(bf16[32,64,256]{2,1,0:T(8,128)(2,1)S(1)} %get-tuple-element.43), channel_id=1, replica_groups=mesh['segment'=4,'blk'=32] {'blk'}, dimensions={0} | all-to-all | bytes 2097152 | tf_op jit(solution)/shard_map/all_to_all | solution.py:188
  356.9 4.6 %all-to-all-start.7 = ((bf16[32,64,256]{2,1,0:T(8,128)(2,1)}), bf16[32,64,256]{2,1,0:T(8,128)(2,1)}, u32[]{:S(2)}, u32[]{:S(2)}) async-start(bf16[32,64,256]{2,1,0:T(8,128)(2,1)} %copy-done.35), calls=%async_computation.7 | async-start | bytes 2097152 | tf_op jit(solution)/shard_map/all_to_all | solution.py:188
  366.2 3.3 shard_map.133
  371.2 7.7 %all-to-all-done.7.arrived = bf16[32,64,256]{2,1,0:T(8,128)(2,1)} async-done(((bf16[32,64,256]{2,1,0:T(8,128)(2,1)}), bf16[32,64,256]{2,1,0:T(8,128)(2,1)}, u32[]{:S(2)}, u32[]{:S(2)}) %all-to-all-start.7) | async-done | bytes 1048608 | tf_op jit(solution)/shard_map/all_to_all | solution.py:188
  378.9 4.0 %all-to-all-start.15 = ((bf16[32,16,256]{2,1,0:T(8,128)(2,1)}), bf16[32,16,256]{2,1,0:T(8,128)(2,1)S(1)}, u32[]{:S(2)}, u32[]{:S(2)}) async-start(bf16[32,16,256]{2,1,0:T(8,128)(2,1)} %copy-done.43), calls=%async_computation.15 | async-start | bytes 524288 | tf_op jit(solution)/shard_map/all_to_all | solution.py:188
  386.4 2.8 shard_map.138
  393.1 3.3 shard_map.137
  (128 shorter events, 74.6 us)
Async XLA Ops:
  5.8 18.2 %all-to-all-start = ((bf16[32,16,256]{2,1,0:T(8,128)(2,1)}), bf16[32,16,256]{2,1,0:T(8,128)(2,1)}, u32[]{:S(2)}, u32[]{:S(2)}) async-start(bf16[32,16,256]{2,1,0:T(8,128)(2,1)} %shard_map.110), calls=%async_computation | async-start | bytes 524288 | tf_op jit(solution)/shard_map/all_to_all | solution.py:188
  24.0 2.2 copy-start.3
  26.2 11.5 %copy-start.10 = (bf16[1,2,1024,256]{3,2,1,0:T(8,128)(2,1)S(1)}, bf16[1,2,1024,256]{3,2,1,0:T(8,128)(2,1)}, u32[]{:S(2)}) copy-start(bf16[1,2,1024,256]{3,2,1,0:T(8,128)(2,1)} %param.11) | copy-start | bytes 3145732
  30.3 24.7 %all-to-all-start.1 = ((bf16[32,64,256]{2,1,0:T(8,128)(2,1)}), bf16[32,64,256]{2,1,0:T(8,128)(2,1)}, u32[]{:S(2)}, u32[]{:S(2)}) async-start(bf16[32,64,256]{2,1,0:T(8,128)(2,1)} %copy-done.28), calls=%async_computation.1 | async-start | bytes 2097152 | tf_op jit(solution)/shard_map/all_to_all | solution.py:188
  58.5 9.1 %collective-permute-start = (bf16[512,256]{1,0:T(8,128)(2,1)}, bf16[512,256]{1,0:T(8,128)(2,1)}, u32[]{:S(2)}, u32[]{:S(2)}) collective-permute-start(bf16[512,256]{1,0:T(8,128)(2,1)} %shard_map.113), channel_id=1, source_target_pairs={{0,32},{1,33},{2,34},{3,35},{4,36},{5,37},{6,38},{7,39},{8,40},{9,... | collective-permute-start | bytes 786440 | tf_op jit(solution)/shard_map/ppermute | solution.py:233
  70.0 38.3 %copy-start.38 = (bf16[512,256]{1,0:T(8,128)(2,1)}, bf16[512,256]{1,0:T(8,128)(2,1)S(1)}, u32[]{:S(2)}) copy-start(bf16[512,256]{1,0:T(8,128)(2,1)S(1)} %get-tuple-element.30.x) | copy-start | bytes 786436
  83.3 2.2 copy-start.4
  85.5 22.8 %copy-start.12 = (bf16[2,256,1024]{2,1,0:T(8,128)(2,1)S(1)}, bf16[2,256,1024]{2,1,0:T(8,128)(2,1)}, u32[]{:S(2)}) copy-start(bf16[2,256,1024]{2,1,0:T(8,128)(2,1)} %copy.14.w4_up) | copy-start | bytes 3145732
  108.7 1.4 collective-permute-start.1
  125.8 2.2 copy-start.5
  128.0 22.8 %copy-start.13 = (bf16[2,256,1024]{2,1,0:T(8,128)(2,1)S(1)}, bf16[2,256,1024]{2,1,0:T(8,128)(2,1)}, u32[]{:S(2)}) copy-start(bf16[2,256,1024]{2,1,0:T(8,128)(2,1)} %copy.14.w4_up) | copy-start | bytes 3145732
  151.9 1.4 collective-permute-start.2
  157.0 13.6 %all-to-all-start.6 = ((bf16[32,16,256]{2,1,0:T(8,128)(2,1)}), bf16[32,16,256]{2,1,0:T(8,128)(2,1)}, u32[]{:S(2)}, u32[]{:S(2)}) async-start(bf16[32,16,256]{2,1,0:T(8,128)(2,1)} %copy-done.44), calls=%async_computation.6 | async-start | bytes 524288 | tf_op jit(solution)/shard_map/all_to_all | solution.py:188
  170.6 21.8 %all-to-all-start.8 = ((bf16[32,64,256]{2,1,0:T(8,128)(2,1)}), bf16[32,64,256]{2,1,0:T(8,128)(2,1)}, u32[]{:S(2)}, u32[]{:S(2)}) async-start(bf16[32,64,256]{2,1,0:T(8,128)(2,1)} %copy-done.27), calls=%async_computation.8 | async-start | bytes 2097152 | tf_op jit(solution)/shard_map/all_to_all | solution.py:188
  175.1 2.2 copy-start.6
  192.5 2.2 copy-start
  194.6 1.6 copy-start.8
  197.5 17.2 %copy-start.21 = (bf16[512,512]{1,0:T(8,128)(2,1)S(1)}, bf16[512,512]{1,0:T(8,128)(2,1)}, u32[]{:S(2)}) copy-start(bf16[512,512]{1,0:T(8,128)(2,1)} %copy-done.20) | copy-start | bytes 1572868
  202.0 34.8 %copy-start.1 = (bf16[1,2,1024,1024]{3,2,1,0:T(8,128)(2,1)S(1)}, bf16[1,2,1024,1024]{3,2,1,0:T(8,128)(2,1)}, u32[]{:S(2)}) copy-start(bf16[1,2,1024,1024]{3,2,1,0:T(8,128)(2,1)} %param.10) | copy-start | bytes 12582916
  214.9 0.7 collective-permute-start.3
  252.8 0.7 collective-permute-start.4
  277.9 83.7 %copy-start.9 = (bf16[512,2048]{1,0:T(8,128)(2,1)S(1)}, bf16[512,2048]{1,0:T(8,128)(2,1)}, u32[]{:S(2)}) copy-start(bf16[512,2048]{1,0:T(8,128)(2,1)} %copy-done.7) | copy-start | bytes 6291460
  291.5 42.0 %collective-permute-start.5 = (bf16[512,256]{1,0:T(8,128)(2,1)}, bf16[512,256]{1,0:T(8,128)(2,1)}, u32[]{:S(2)}, u32[]{:S(2)}) collective-permute-start(bf16[512,256]{1,0:T(8,128)(2,1)} %shard_map.131), channel_id=1, source_target_pairs={{32,0},{33,1},{34,2},{35,3},{36,4},{37,5},{38,6},{39,7},{40,8},{41... | collective-permute-start | bytes 786440 | tf_op jit(solution)/shard_map/ppermute | solution.py:260
  356.9 22.0 %all-to-all-start.7 = ((bf16[32,64,256]{2,1,0:T(8,128)(2,1)}), bf16[32,64,256]{2,1,0:T(8,128)(2,1)}, u32[]{:S(2)}, u32[]{:S(2)}) async-start(bf16[32,64,256]{2,1,0:T(8,128)(2,1)} %copy-done.35), calls=%async_computation.7 | async-start | bytes 2097152 | tf_op jit(solution)/shard_map/all_to_all | solution.py:188
  361.6 2.2 copy-start.2
  366.2 16.7 %copy-start.14 = (bf16[2,256,1024]{2,1,0:T(8,128)(2,1)S(1)}, bf16[2,256,1024]{2,1,0:T(8,128)(2,1)}, u32[]{:S(2)}) copy-start(bf16[2,256,1024]{2,1,0:T(8,128)(2,1)} %copy.14.w4_up) | copy-start | bytes 3145732
  366.2 16.8 %copy-start.30 = (bf16[512,256]{1,0:T(8,128)(2,1)S(1)}, bf16[512,256]{1,0:T(8,128)(2,1)}, u32[]{:S(2)}) copy-start(bf16[512,256]{1,0:T(8,128)(2,1)} %copy-done.29) | copy-start | bytes 786436
  378.9 14.3 %copy-start.19 = (bf16[32,64,256]{2,1,0:T(8,128)(2,1)S(1)}, bf16[32,64,256]{2,1,0:T(8,128)(2,1)}, u32[]{:S(2)}) copy-start(bf16[32,64,256]{2,1,0:T(8,128)(2,1)} %all_to_all.89.arrived.back) | copy-start | bytes 3145732
  378.9 17.6 %all-to-all-start.15 = ((bf16[32,16,256]{2,1,0:T(8,128)(2,1)}), bf16[32,16,256]{2,1,0:T(8,128)(2,1)S(1)}, u32[]{:S(2)}, u32[]{:S(2)}) async-start(bf16[32,16,256]{2,1,0:T(8,128)(2,1)} %copy-done.43), calls=%async_computation.15 | async-start | bytes 524288 | tf_op jit(solution)/shard_map/all_to_all | solution.py:188
  386.4 6.7 %copy-start.41 = (bf16[2,1024,256]{2,1,0:T(8,128)(2,1)S(1)}, bf16[2,1024,256]{2,1,0:T(8,128)(2,1)}, u32[]{:S(2)}) copy-start(bf16[2,1024,256]{2,1,0:T(8,128)(2,1)} %copy-done.40) | copy-start | bytes 3145732
  390.4 6.1 %copy-start.22 = (bf16[512,512]{1,0:T(8,128)(2,1)S(1)}, bf16[512,512]{1,0:T(8,128)(2,1)}, u32[]{:S(2)}) copy-start(bf16[512,512]{1,0:T(8,128)(2,1)} %copy-done.20) | copy-start | bytes 1572868
  390.4 6.1 %copy-start.33 = (bf16[512,256]{1,0:T(8,128)(2,1)S(1)}, bf16[512,256]{1,0:T(8,128)(2,1)}, u32[]{:S(2)}) copy-start(bf16[512,256]{1,0:T(8,128)(2,1)} %copy-done.31) | copy-start | bytes 786436
  (25 other events, 25.0 us)

commit v2 on v1

v2 whole, which is shorter than its diff:
```python
import functools

import jax
import jax.numpy as jnp
from jax import lax
from jax.experimental import pallas as pl
from jax.experimental.pallas import tpu as pltpu
from jax.sharding import PartitionSpec as P

VMEM_BYTES = 12 * 1024 * 1024
BF16 = jnp.bfloat16
F32 = jnp.float32
CUBIC = 0.044715
ROOT = 0.7978845608028654
COUNT = 256
PEERS = 32
FLAT = (512, COUNT)
CHUNK = (PEERS, 16, COUNT)
WIDE = (PEERS, 64, COUNT)
INNER = (2, 1024, COUNT)
PARTS = (2, 256, COUNT)


class Near:
    def __init__(self, value):
        self.value = value


class Far:
    def __init__(self, value):
        self.value = value


def call(body, outs, *args, scratch=()):
    place = pl.BlockSpec(memory_space=pltpu.VMEM)
    scalar = pl.BlockSpec(memory_space=pltpu.SMEM)
    specs, operands = [], []
    for arg in args:
        if isinstance(arg, Near):
            specs.append(place)
            operands.append(pltpu.with_memory_space_constraint(arg.value, pltpu.VMEM))
        elif isinstance(arg, Far):
            specs.append(pl.BlockSpec(memory_space=pltpu.HBM))
            operands.append(pltpu.with_memory_space_constraint(arg.value, pltpu.HBM))
        else:
            specs.append(scalar if arg.dtype == jnp.int32 else place)
            operands.append(arg)
    shapes = [
        pltpu.VMEM(out.value, BF16) if isinstance(out, Near) else jax.ShapeDtypeStruct(out, BF16)
        for out in outs
    ]
    return pl.pallas_call(
        body,
        out_shape=shapes,
        in_specs=specs,
        out_specs=[place] * len(outs),
        scratch_shapes=list(scratch),
        compiler_params=pltpu.CompilerParams(vmem_limit_bytes=VMEM_BYTES),
    )(*operands)


def load_body(*refs):
    sources, plain, turned_refs, done = refs[0:4], refs[4:8], refs[8:12], refs[12]
    copies = [
        pltpu.make_async_copy(source, target, done.at[i])
        for i, (source, target) in enumerate(zip(sources, plain))
    ]
    for copy in copies:
        copy.start()
    for copy, source, target in zip(copies, plain, turned_refs):
        copy.wait()
        for b in range(2):
            target[b] = source[b].T


def load(*weights):
    shapes = [w.shape for w in weights]
    shapes += [(w.shape[0], w.shape[2], w.shape[1]) for w in weights]
    return pl.pallas_call(
        load_body,
        out_shape=[pltpu.VMEM(shape, BF16) for shape in shapes],
        in_specs=[pl.BlockSpec(memory_space=pltpu.HBM)] * 4,
        out_specs=[pl.BlockSpec(memory_space=pltpu.VMEM)] * 8,
        scratch_shapes=[pltpu.SemaphoreType.DMA((4,))],
        compiler_params=pltpu.CompilerParams(vmem_limit_bytes=VMEM_BYTES),
    )(*[pltpu.with_memory_space_constraint(w, pltpu.HBM) for w in weights])


def dot(left, right):
    return lax.dot_general(left, right, (((1,), (0,)), ((), ())), preferred_element_type=F32)


def dot_nt(left, right):
    return lax.dot_general(left, right, (((1,), (1,)), ((), ())), preferred_element_type=F32)


def upper_rows(shape):
    return lax.rem(lax.broadcasted_iota(jnp.int32, shape, 0), 8) < 4


def interleave(a, b):
    upper = upper_rows(a.shape)
    first = jnp.where(upper, a, pltpu.roll(b, 4, 0))
    second = jnp.where(upper, pltpu.roll(a, 252, 0), b)
    return stack_halves(first, second)


def stack_halves(first, second):
    tiles = [item.reshape(PEERS, 1, 8, COUNT) for item in (first, second)]
    return jnp.concatenate(tiles, axis=1).reshape(CHUNK).astype(BF16)


def halves_of(joined):
    tiles = joined.astype(F32).reshape(PEERS, 2, 8, COUNT)
    return [tiles[:, g].reshape(256, COUNT) for g in range(2)]


def separate(joined):
    first, second = halves_of(joined)
    upper = upper_rows(first.shape)
    a = jnp.where(upper, first, pltpu.roll(second, 4, 0))
    b = jnp.where(upper, pltpu.roll(first, 252, 0), second)
    return a.astype(BF16), b.astype(BF16)


def enter(tokens, w1_up, x, mixed):
    x[...] = tokens[...].T
    mixed[...] = interleave(*[dot(w1_up[k], x[256 * k : 256 * (k + 1), :]) for k in range(2)])


def gelu_tanh(value):
    return jnp.tanh(ROOT * (value + CUBIC * (value * value * value)))


def gelu(value):
    return 0.5 * value * (1.0 + gelu_tanh(value))


def gelu_slope(value):
    bend = gelu_tanh(value)
    slope = ROOT * (1.0 + 3.0 * CUBIC * (value * value))
    return 0.5 * (1.0 + bend) + (0.5 * value * (1.0 - bend * bend)) * slope


def middle(arrived, w2_up, w3_up, spread, *kept):
    joined = [half.astype(BF16) for half in halves_of(arrived[...])]
    for g in range(2):
        pre = dot(w2_up[g], joined[g]).astype(BF16)
        act = gelu(pre.astype(F32)).astype(BF16)
        if kept:
            kept[0][g] = pre
            kept[1][g] = act
        out = dot(w3_up[g], act).astype(BF16)
        spread[:, 32 * g : 32 * (g + 1), :] = out.reshape(PEERS, 32, COUNT)


def middle_or_first(plane, here, arrived, w2_up, w3_up, far_tokens, w4, spread, up, tokens, done):
    @pl.when(here[0] == plane)
    def _():
        copy = pltpu.make_async_copy(far_tokens, tokens, done)
        copy.start()
        copy.wait()
        up[...] = tokens[...].T
        back_spread(up, w4, spread)

    @pl.when(here[0] != plane)
    def _():
        up[...] = jnp.zeros_like(up)
        middle(arrived, w2_up, w3_up, spread)


def leave_rows(arrived, w4_up, x, out):
    rows = arrived[...].reshape(64, 32, COUNT)
    for k in range(2):
        part = rows[:, 16 * k : 16 * (k + 1), :].reshape(1024, COUNT)
        place = slice(256 * k, 256 * (k + 1))
        out[place, :] = (x[place, :].astype(F32) + dot(w4_up[k], part)).astype(BF16)


def leave(arrived, x, w4_up, out):
    leave_rows(arrived, w4_up, x, out)


def enter_choice(plane, here, incoming, held, w1_up, x, mixed):
    x[...] = jnp.where(here[0] == plane, incoming[...], held[...])
    mixed[...] = interleave(*[dot(w1_up[k], x[256 * k : 256 * (k + 1), :]) for k in range(2)])


def back_spread(up, w4, spread):
    parts = []
    for k in range(2):
        part = dot(w4[k], up[256 * k : 256 * (k + 1), :]).astype(BF16)
        parts.append(part.reshape(64, 1, 16, COUNT))
    spread[...] = jnp.concatenate(parts, axis=1).reshape(WIDE)


def unmix(joined, w1, up, out):
    for k, part in enumerate(separate(joined)):
        rows = slice(256 * k, 256 * (k + 1))
        out[rows, :] = (up[rows, :].astype(F32) + dot(w1[k], part)).astype(BF16)


def back_enter_choice(plane, here, incoming, held, w4, up, spread):
    up[...] = jnp.where(here[0] == plane, incoming[...], held[...])
    back_spread(up, w4, spread)


def back_enter_or_last(plane, here, ready, incoming, held, w4, up, spread):
    @pl.when(here[0] == plane + 1)
    def _():
        up[...] = held[...]
        spread[...] = ready[...]

    @pl.when(here[0] != plane + 1)
    def _():
        back_enter_choice(plane, here, incoming, held, w4, up, spread)


def back_step(arrived, up, w1, out):
    unmix(arrived[...], w1, up, out)


def back_leave(arrived, up, w1, out, parts):
    for k, part in enumerate(separate(arrived[...])):
        parts[k] = part
        rows = slice(256 * k, 256 * (k + 1))
        total = up[rows, :].astype(F32) + dot(w1[k], part)
        out[:, rows] = total.astype(BF16).T


def back_middle(arrived, pre, w2, w3, back, *kept):
    terms = []
    for g in range(2):
        part = arrived[:, 32 * g : 32 * (g + 1), :].reshape(1024, COUNT)
        grad_pre = (dot(w3[g], part) * gelu_slope(pre[g].astype(F32))).astype(BF16)
        if kept:
            kept[0][g] = grad_pre
        terms.append(dot(w2[g], grad_pre))
    back[...] = stack_halves(*terms)


def leave_and_fourth(plane, here, rows_new, rows_held, x, w4_up, up, out, grad):
    rows = jnp.where(here[0] == plane, rows_new[...], rows_held[...])
    rows = rows.reshape(64, 32, COUNT)
    for k in range(2):
        part = rows[:, 16 * k : 16 * (k + 1), :].reshape(1024, COUNT)
        place = slice(256 * k, 256 * (k + 1))
        total = x[place, :].astype(F32) + dot(w4_up[k], part)
        out[:, place] = total.astype(BF16).T
        grad[k] = dot_nt(part, up[place, :]).astype(BF16)


def grads_third(act, back, grad):
    for g in range(2):
        part = back[:, 32 * g : 32 * (g + 1), :].reshape(1024, COUNT)
        for start in range(0, 1024, 256):
            rows = slice(start, start + 256)
            grad[g, rows, :] = dot_nt(act[g, rows, :], part).astype(BF16)


def grads_second(mixed, pre, grad):
    for g, part in enumerate(halves_of(mixed[...])):
        grad[g] = dot_nt(part.astype(BF16), pre[g]).astype(BF16)


def grads_first(x, back, grad):
    for k in range(2):
        grad[k] = dot_nt(x[256 * k : 256 * (k + 1), :], back[k]).astype(BF16)


def exchange(block):
    return lax.all_to_all(block, "blk", split_axis=0, concat_axis=0, tiled=True)


def shards(tokens, cotangent, first_factor, second_factor, third_factor, fourth_factor):
    segments = lax.axis_size("segment")
    position = lax.axis_index("segment")
    own = (first_factor[0], second_factor[0], third_factor[0], fourth_factor[0])

    here = position.astype(jnp.int32).reshape(1)
    tokens, here = lax.optimization_barrier((tokens, here))
    w1, w2, w3, w4, w1_up, w2_up, w3_up, w4_up = [Near(item) for item in load(*own)]

    for step in range(segments):
        if step == 0:
            x, mixed = call(enter, [Near(FLAT), Near(CHUNK)], tokens, w1_up)
        else:
            x, mixed = call(
                functools.partial(enter_choice, step),
                [Near(FLAT), Near(CHUNK)],
                here,
                Near(incoming),
                Near(x),
                w1_up,
            )
        arrived = exchange(mixed)
        if step < segments - 2:
            (spread,) = call(middle, [Near(WIDE)], Near(arrived), w2_up, w3_up)
        elif step == segments - 2:
            spread, up = call(
                functools.partial(middle_or_first, segments - 1),
                [Near(WIDE), Near(FLAT)],
                here,
                Near(arrived),
                w2_up,
                w3_up,
                Far(cotangent),
                w4,
                scratch=[pltpu.VMEM((COUNT, 512), BF16), pltpu.SemaphoreType.DMA],
            )
        else:
            spread, pre, act = call(
                middle,
                [Near(WIDE), Near(INNER), Near(INNER)],
                Near(arrived),
                w2_up,
                w3_up,
            )
            break
        rows = exchange(spread)
        (out,) = call(leave, [Near(FLAT)], Near(rows), Near(x), w4_up)
        incoming = lax.ppermute(out, "segment", [(step, step + 1)])

    mixed_in, gathered = arrived, rows
    for step in range(segments):
        last = step == segments - 1
        plane = segments - 1 - step
        if step == 1:
            up, spread = call(
                functools.partial(back_enter_or_last, plane),
                [Near(FLAT), Near(WIDE)],
                here,
                Near(spread),
                Near(incoming),
                Near(up),
                w4,
            )
            rows_last = gathered = exchange(spread)
        elif step:
            up, spread = call(
                functools.partial(back_enter_choice, plane),
                [Near(FLAT), Near(WIDE)],
                here,
                Near(incoming),
                Near(up),
                w4,
            )
            gathered = exchange(spread)
        shapes = [CHUNK, INNER] if last else [Near(CHUNK)]
        results = call(back_middle, shapes, Near(gathered), Near(pre), w2, w3)
        arrived = exchange(results[0])
        if not last:
            (grad_in,) = call(back_step, [Near(FLAT)], Near(arrived), Near(up), w1)
            incoming = lax.ppermute(grad_in, "segment", [(plane, plane - 1)])

    grad_pre = results[1]
    segment_outputs, fourth_grad = call(
        functools.partial(leave_and_fourth, segments - 1),
        [(COUNT, 512), own[3].shape],
        here,
        rows_last,
        rows,
        x,
        w4_up,
        up,
    )
    (third_grad,) = call(grads_third, [own[2].shape], act, gathered)
    (second_grad,) = call(grads_second, [own[1].shape], mixed_in, grad_pre)
    grad_in, parts = call(back_leave, [(COUNT, 512), PARTS], arrived, up, own[0])
    (first_grad,) = call(grads_first, [own[0].shape], x, parts)
    return (
        segment_outputs[None],
        grad_in[None],
        first_grad[None],
        second_grad[None],
        third_grad[None],
        fourth_grad[None],
    )


def solution(mesh):
    placed = (
        P(None, "blk"),
        P(None, "blk"),
        P("segment", "blk", None, None),
        P("segment", "blk", None, None),
        P("segment", "blk", None, None),
        P("segment", "blk", None, None),
    )
    return jax.shard_map(
        shards,
        mesh=mesh,
        in_specs=placed,
        out_specs=(
            P("segment", None, "blk"),
            P("segment", None, "blk"),
            P("segment", "blk", None, None),
            P("segment", "blk", None, None),
            P("segment", "blk", None, None),
            P("segment", "blk", None, None),
        ),
        check_vma=False,
    )
```

time: 401 us -> 322 us (0.80)
  blocking collectives: 168 us -> 218 us
  local copies, waits for them, and re-layouts: 51 us -> 5.53 us
  waiting for transfers between devices: 84.8 us -> 46.3 us
  starting transfers between devices: 43.5 us -> 12.1 us
  Pallas kernels: 50.9 us -> 39.1 us
    all_to_all x10 -> x13, blocking collectives: 168 us -> 218 us  [exchange(): return lax.all_to_all(block, 'blk', split_axis=0, concat_axis=0, tiled=True)]
    all_to_all x6 -> x1, waiting for transfers between devices: 39.3 us -> 0.01 us  [exchange(): return lax.all_to_all(block, 'blk', split_axis=0, concat_axis=0, tiled=True)]
    unnamed x94 -> x30, local copies, waits for them, and re-layouts: 43.5 us -> 5.53 us
    all_to_all x6 -> x1, starting transfers between devices: 33.8 us -> 4.56 us  [exchange(): return lax.all_to_all(block, 'blk', split_axis=0, concat_axis=0, tiled=True)]
    pallas_call x30 -> x27, Pallas kernels: 50.9 us -> 39.1 us  [the longest x26 34.8 us: call(): pl.pallas_call(body, out_shape=shapes, in_specs=specs, out_specs=[place]...]
    transpose x2 -> x0, local copies, waits for them, and re-layouts: 7.5 us -> none  [the longest x1 6.19 us: shards(): w3_up = w3.transpose(0, 2, 1)]
  transfers between devices with their start and end apart: 12 -> 7, of which waited for: 6 -> 2; matrix products, arithmetic and copies ran while one was open for 2% -> 0% of each run, Pallas kernels for 5% -> 2%
where the time goes in v2:
time: 322 us
  blocking collectives  218 us (68%)
  waiting for transfers between devices  46.3 us (14%)
  Pallas kernels  39.1 us (12%)
  starting transfers between devices  12.1 us (4%)
  local copies, waits for them, and re-layouts  5.53 us (2%)
    all_to_all x13, blocking collectives, exchange(): return lax.all_to_all(block, 'blk', split_axis=0, concat_axis=0, tiled=True)  218 us
    ppermute x3, waiting for transfers between devices, shards(): incoming = lax.ppermute(grad_in, 'segment', [(plane, plane - 1)])  41 us
    pallas_call x26, Pallas kernels, call(): pl.pallas_call(body, out_shape=shapes, in_specs=specs, out_specs=[place]...  34.8 us
  transfers between devices with their start and end apart: 7, of which 2 were waited for; matrix products, arithmetic and copies ran while one was open for 0% of the time, Pallas kernels for 2%

profile of v2, /device:TPU:1, one launch (start us, length us, event | category | flops | bytes accessed | tf_op | source)
XLA Modules:
  0.0 321.5 jit_solution(16080016921717490389)
XLA Ops:
  0.6 4.2 %shard_map.109 = (bf16[2,256,256]{2,1,0:T(8,128)(2,1)S(1)}, bf16[2,256,1024]{2,1,0:T(8,128)(2,1)S(1)}, bf16[2,1024,1024]{2,1,0:T(8,128)(2,1)S(1)}, bf16[2,1024,2...) custom-call(bf16[2,256,256]{2,1,0:T(8,128)(2,1)} %bitcast.11, ...), custom_call_target="tpu_custom_call" | custom-call | tf_op jit(solution)/shard_map/pallas_call | solution.py:79
  5.2 17.3 %all_to_all.70.arrived = bf16[32,16,256]{2,1,0:T(8,128)(2,1)S(1)} all-to-all(bf16[32,16,256]{2,1,0:T(8,128)(2,1)S(1)} %get-tuple-element.44), channel_id=1, replica_groups=mesh['segment'=4,'blk'=32] {'blk'}, dimensions={0} | all-to-all | bytes 524288 | tf_op jit(solution)/shard_map/all_to_all | solution.py:272
  22.5 1.8 shard_map.111
  24.3 20.7 %all_to_all.71.arrived = bf16[32,64,256]{2,1,0:T(8,128)(2,1)S(1)} all-to-all(bf16[32,64,256]{2,1,0:T(8,128)(2,1)S(1)} %shard_map.111), channel_id=1, replica_groups=mesh['segment'=4,'blk'=32] {'blk'}, dimensions={0} | all-to-all | bytes 2097152 | tf_op jit(solution)/shard_map/all_to_all | solution.py:272
  45.5 3.6 %collective-permute-start = (bf16[512,256]{1,0:T(8,128)(2,1)S(1)}, bf16[512,256]{1,0:T(8,128)(2,1)S(1)}, u32[]{:S(2)}, u32[]{:S(2)}) collective-permute-start(bf16[512,256]{1,0:T(8,128)(2,1)S(1)} %shard_map.112), channel_id=1, source_target_pairs={{0,32},{1,33},{2,34},{3,35},{4,36},{5,37},{6,38},{7,39},{8,40},{9,... | collective-permute-start | bytes 786440 | tf_op jit(solution)/shard_map/ppermute | solution.py:322
  49.1 5.3 %collective-permute-done.incoming = bf16[512,256]{1,0:T(8,128)(2,1)S(1)} collective-permute-done((bf16[512,256]{1,0:T(8,128)(2,1)S(1)}, bf16[512,256]{1,0:T(8,128)(2,1)S(1)}, u32[]{:S(2)}, u32[]{:S(2)}) %collective-permute-start) | collective-permute-done | bytes 262176 | tf_op jit(solution)/shard_map/ppermute | solution.py:322
  54.6 13.3 %all_to_all.72.arrived = bf16[32,16,256]{2,1,0:T(8,128)(2,1)S(1)} all-to-all(bf16[32,16,256]{2,1,0:T(8,128)(2,1)S(1)} %get-tuple-element.49), channel_id=1, replica_groups=mesh['segment'=4,'blk'=32] {'blk'}, dimensions={0} | all-to-all | bytes 524288 | tf_op jit(solution)/shard_map/all_to_all | solution.py:272
  67.9 1.8 shard_map.114
  69.7 20.7 %all_to_all.73.arrived = bf16[32,64,256]{2,1,0:T(8,128)(2,1)S(1)} all-to-all(bf16[32,64,256]{2,1,0:T(8,128)(2,1)S(1)} %shard_map.114), channel_id=1, replica_groups=mesh['segment'=4,'blk'=32] {'blk'}, dimensions={0} | all-to-all | bytes 2097152 | tf_op jit(solution)/shard_map/all_to_all | solution.py:272
  91.8 12.4 %all_to_all.74.arrived = bf16[32,16,256]{2,1,0:T(8,128)(2,1)S(1)} all-to-all(bf16[32,16,256]{2,1,0:T(8,128)(2,1)S(1)} %get-tuple-element.51), channel_id=1, replica_groups=mesh['segment'=4,'blk'=32] {'blk'}, dimensions={0} | all-to-all | bytes 524288 | tf_op jit(solution)/shard_map/all_to_all | solution.py:272
  104.3 1.8 shard_map.117
  106.1 20.7 %all_to_all.75.arrived.rows_held = bf16[32,64,256]{2,1,0:T(8,128)(2,1)S(1)} all-to-all(bf16[32,64,256]{2,1,0:T(8,128)(2,1)S(1)} %get-tuple-element.53), channel_id=1, replica_groups=mesh['segment'=4,'blk'=32] {'blk'}, dimensions={0} | all-to-all | bytes 2097152 | tf_op jit(solution)/shard_map/all_to_all | solution.py:272
  128.2 12.4 %all_to_all.76.arrived.mixed = bf16[32,16,256]{2,1,0:T(8,128)(2,1)S(1)} all-to-all(bf16[32,16,256]{2,1,0:T(8,128)(2,1)S(1)} %get-tuple-element.55), channel_id=1, replica_groups=mesh['segment'=4,'blk'=32] {'blk'}, dimensions={0} | all-to-all | bytes 524288 | tf_op jit(solution)/shard_map/all_to_all | solution.py:272
  140.7 1.9 shard_map.120
  142.5 3.4 %shard_map.121 = bf16[32,16,256]{2,1,0:T(8,128)(2,1)S(1)} custom-call(bf16[32,64,256]{2,1,0:T(8,128)(2,1)S(1)} %all_to_all.75.arrived.rows_held, bf16[2,1024,256]{2,1,0:T(8,128)(2,1)S(1)} %get-tuple-element.57.pre, bf16[2,256,1024]{2,1,0:T(8,128)(2,1)S(1)} %get-tuple-element.58.w2, bf16[2,1024,1024]{2,1,0:T(8,128)(2,1)S(1)} %get-tuple-element.59.w3), custom_call_target="tpu_custom_call" | custom-call | tf_op jit(solution)/shard_map/pallas_call | solution.py:52
  145.9 12.4 %all_to_all.77.arrived = bf16[32,16,256]{2,1,0:T(8,128)(2,1)S(1)} all-to-all(bf16[32,16,256]{2,1,0:T(8,128)(2,1)S(1)} %shard_map.121), channel_id=1, replica_groups=mesh['segment'=4,'blk'=32] {'blk'}, dimensions={0} | all-to-all | bytes 524288 | tf_op jit(solution)/shard_map/all_to_all | solution.py:272
  159.8 20.7 %all_to_all.78.arrived.rows_new = bf16[32,64,256]{2,1,0:T(8,128)(2,1)S(1)} all-to-all(bf16[32,64,256]{2,1,0:T(8,128)(2,1)S(1)} %get-tuple-element.62), channel_id=1, replica_groups=mesh['segment'=4,'blk'=32] {'blk'}, dimensions={0} | all-to-all | bytes 2097152 | tf_op jit(solution)/shard_map/all_to_all | solution.py:272
  180.6 3.4 %shard_map.124 = bf16[32,16,256]{2,1,0:T(8,128)(2,1)S(1)} custom-call(bf16[32,64,256]{2,1,0:T(8,128)(2,1)S(1)} %all_to_all.78.arrived.rows_new, bf16[2,1024,256]{2,1,0:T(8,128)(2,1)S(1)} %get-tuple-element.57.pre, bf16[2,256,1024]{2,1,0:T(8,128)(2,1)S(1)} %get-tuple-element.58.w2, bf16[2,1024,1024]{2,1,0:T(8,128)(2,1)S(1)} %get-tuple-element.59.w3), custom_call_target="tpu_custom_call" | custom-call | tf_op jit(solution)/shard_map/pallas_call | solution.py:52
  183.9 12.4 %all_to_all.79.arrived = bf16[32,16,256]{2,1,0:T(8,128)(2,1)S(1)} all-to-all(bf16[32,16,256]{2,1,0:T(8,128)(2,1)S(1)} %shard_map.124), channel_id=1, replica_groups=mesh['segment'=4,'blk'=32] {'blk'}, dimensions={0} | all-to-all | bytes 524288 | tf_op jit(solution)/shard_map/all_to_all | solution.py:272
  197.8 20.7 %all_to_all.80.arrived = bf16[32,64,256]{2,1,0:T(8,128)(2,1)S(1)} all-to-all(bf16[32,64,256]{2,1,0:T(8,128)(2,1)S(1)} %get-tuple-element.65), channel_id=1, replica_groups=mesh['segment'=4,'blk'=32] {'blk'}, dimensions={0} | all-to-all | bytes 2097152 | tf_op jit(solution)/shard_map/all_to_all | solution.py:272
  218.5 3.4 %shard_map.127 = bf16[32,16,256]{2,1,0:T(8,128)(2,1)S(1)} custom-call(bf16[32,64,256]{2,1,0:T(8,128)(2,1)S(1)} %all_to_all.80.arrived, bf16[2,1024,256]{2,1,0:T(8,128)(2,1)S(1)} %get-tuple-element.57.pre, bf16[2,256,1024]{2,1,0:T(8,128)(2,1)S(1)} %get-tuple-element.58.w2, bf16[2,1024,1024]{2,1,0:T(8,128)(2,1)S(1)} %get-tuple-element.59.w3), custom_call_target="tpu_custom_call" | custom-call | tf_op jit(solution)/shard_map/pallas_call | solution.py:52
  221.9 12.4 %all_to_all.81.arrived = bf16[32,16,256]{2,1,0:T(8,128)(2,1)S(1)} all-to-all(bf16[32,16,256]{2,1,0:T(8,128)(2,1)S(1)} %shard_map.127), channel_id=1, replica_groups=mesh['segment'=4,'blk'=32] {'blk'}, dimensions={0} | all-to-all | bytes 524288 | tf_op jit(solution)/shard_map/all_to_all | solution.py:272
  234.6 1.3 collective-permute-start.5
  235.9 41.0 %collective-permute-done.5.incoming = bf16[512,256]{1,0:T(8,128)(2,1)S(1)} collective-permute-done((bf16[512,256]{1,0:T(8,128)(2,1)S(1)}, bf16[512,256]{1,0:T(8,128)(2,1)S(1)}, u32[]{:S(2)}, u32[]{:S(2)}) %collective-permute-start.5) | collective-permute-done | bytes 262176 | tf_op jit(solution)/shard_map/ppermute | solution.py:354
  278.0 21.1 %all_to_all.82.arrived.back = bf16[32,64,256]{2,1,0:T(8,128)(2,1)S(1)} all-to-all(bf16[32,64,256]{2,1,0:T(8,128)(2,1)S(1)} %get-tuple-element.69), channel_id=1, replica_groups=mesh['segment'=4,'blk'=32] {'blk'}, dimensions={0} | all-to-all | bytes 2097152 | tf_op jit(solution)/shard_map/all_to_all | solution.py:272
  299.2 3.4 %shard_map.131 = (bf16[32,16,256]{2,1,0:T(8,128)(2,1)S(1)}, bf16[2,1024,256]{2,1,0:T(8,128)(2,1)S(1)}) custom-call(bf16[32,64,256]{2,1,0:T(8,128)(2,1)S(1)} %all_to_all.82.arrived.back, bf16[2,1024,256]{2,1,0:T(8,128)(2,1)S(1)} %get-tuple-element.57.pre, bf16[2,256,1024]{2,1,0:T(8,128)(2,1)S(1)} %get-tuple-element.58.w2, ...), custom_call_target="tpu_custom_call" | custom-call | tf_op jit(solution)/shard_map/pallas_call | solution.py:52
  304.3 4.6 %all-to-all-start.13 = ((bf16[32,16,256]{2,1,0:T(8,128)(2,1)}), bf16[32,16,256]{2,1,0:T(8,128)(2,1)}, u32[]{:S(2)}, u32[]{:S(2)}) async-start(bf16[32,16,256]{2,1,0:T(8,128)(2,1)} %copy-done.14), calls=%async_computation.13 | async-start | bytes 524288 | tf_op jit(solution)/shard_map/all_to_all | solution.py:272
  308.8 1.2 copy-done.1
  312.0 1.8 shard_map.130
  313.8 1.4 shard_map.134
  315.2 3.3 %shard_map.135 = bf16[2,1024,1024]{2,1,0:T(8,128)(2,1)} custom-call(bf16[2,1024,256]{2,1,0:T(8,128)(2,1)S(1)} %copy-done.6, bf16[32,64,256]{2,1,0:T(8,128)(2,1)S(1)} %all_to_all.82.arrived.back), custom_call_target="tpu_custom_call" | custom-call | tf_op jit(solution)/shard_map/pallas_call | solution.py:52
  318.5 2.0 shard_map.132
  (52 shorter events, 12.6 us)
Async XLA Ops:
  0.6 4.3 %copy-start.13 = (bf16[256,512]{1,0:T(8,128)(2,1)S(1)}, bf16[256,512]{1,0:T(8,128)(2,1)}, u32[]{:S(2)}) copy-start(bf16[256,512]{1,0:T(8,128)(2,1)} %tokens) | copy-start | bytes 786436
  45.5 8.8 %collective-permute-start = (bf16[512,256]{1,0:T(8,128)(2,1)S(1)}, bf16[512,256]{1,0:T(8,128)(2,1)S(1)}, u32[]{:S(2)}, u32[]{:S(2)}) collective-permute-start(bf16[512,256]{1,0:T(8,128)(2,1)S(1)} %shard_map.112), channel_id=1, source_target_pairs={{0,32},{1,33},{2,34},{3,35},{4,36},{5,37},{6,38},{7,39},{8,40},{9,... | collective-permute-start | bytes 786440 | tf_op jit(solution)/shard_map/ppermute | solution.py:322
  90.9 0.7 collective-permute-start.1
  127.3 0.7 collective-permute-start.2
  128.2 17.7 %copy-start.7 = (bf16[512,256]{1,0:T(8,128)(2,1)}, bf16[512,256]{1,0:T(8,128)(2,1)S(1)}, u32[]{:S(2)}) copy-start(bf16[512,256]{1,0:T(8,128)(2,1)S(1)} %get-tuple-element.63.x) | copy-start | bytes 786436
  142.5 16.1 %copy-start.5 = (bf16[2,1024,256]{2,1,0:T(8,128)(2,1)}, bf16[2,1024,256]{2,1,0:T(8,128)(2,1)S(1)}, u32[]{:S(2)}) copy-start(bf16[2,1024,256]{2,1,0:T(8,128)(2,1)S(1)} %get-tuple-element.74.act) | copy-start | bytes 3145732
  158.7 0.7 collective-permute-start.3
  180.6 16.1 %copy-start = (bf16[32,64,256]{2,1,0:T(8,128)(2,1)}, bf16[32,64,256]{2,1,0:T(8,128)(2,1)S(1)}, u32[]{:S(2)}) copy-start(bf16[32,64,256]{2,1,0:T(8,128)(2,1)S(1)} %all_to_all.78.arrived.rows_new) | copy-start | bytes 3145732
  196.6 0.7 collective-permute-start.4
  234.6 42.3 %collective-permute-start.5 = (bf16[512,256]{1,0:T(8,128)(2,1)S(1)}, bf16[512,256]{1,0:T(8,128)(2,1)S(1)}, u32[]{:S(2)}, u32[]{:S(2)}) collective-permute-start(bf16[512,256]{1,0:T(8,128)(2,1)S(1)} %shard_map.128), channel_id=1, source_target_pairs={{32,0},{33,1},{34,2},{35,3},{36,4},{37,5},{38,6},{39,7},{40,8},{41... | collective-permute-start | bytes 786440 | tf_op jit(solution)/shard_map/ppermute | solution.py:354
  277.3 0.7 copy-start.10
  302.6 1.0 copy-start.3
  303.6 0.7 copy-start.14
  304.3 14.3 %all-to-all-start.13 = ((bf16[32,16,256]{2,1,0:T(8,128)(2,1)}), bf16[32,16,256]{2,1,0:T(8,128)(2,1)}, u32[]{:S(2)}, u32[]{:S(2)}) async-start(bf16[32,16,256]{2,1,0:T(8,128)(2,1)} %copy-done.14), calls=%async_computation.13 | async-start | bytes 524288 | tf_op jit(solution)/shard_map/all_to_all | solution.py:272
  308.8 1.2 copy-start.1
  310.1 0.9 copy-start.8
  311.0 0.9 copy-start.11
  312.0 1.8 copy-start.4
  312.0 3.2 %copy-start.6 = (bf16[2,1024,256]{2,1,0:T(8,128)(2,1)S(1)}, bf16[2,1024,256]{2,1,0:T(8,128)(2,1)}, u32[]{:S(2)}) copy-start(bf16[2,1024,256]{2,1,0:T(8,128)(2,1)} %copy-done.5) | copy-start | bytes 3145732
  313.7 4.8 %copy-start.2 = (bf16[1,2,256,256]{3,2,1,0:T(8,128)(2,1)S(1)}, bf16[1,2,256,256]{3,2,1,0:T(8,128)(2,1)}, u32[]{:S(2)}) copy-start(bf16[1,2,256,256]{3,2,1,0:T(8,128)(2,1)} %param.8) | copy-start | bytes 786436
  313.7 4.8 %copy-start.12 = (bf16[512,256]{1,0:T(8,128)(2,1)S(1)}, bf16[512,256]{1,0:T(8,128)(2,1)}, u32[]{:S(2)}) copy-start(bf16[512,256]{1,0:T(8,128)(2,1)} %copy-done.10) | copy-start | bytes 786436
  313.8 6.8 %copy-start.9 = (bf16[512,256]{1,0:T(8,128)(2,1)S(1)}, bf16[512,256]{1,0:T(8,128)(2,1)}, u32[]{:S(2)}) copy-start(bf16[512,256]{1,0:T(8,128)(2,1)} %copy-done.7) | copy-start | bytes 786436

commit v3 on v2

--- a/solution.py
+++ b/solution.py
@@ -22,8 +22,9 @@
 
 
 class Near:
-    def __init__(self, value):
+    def __init__(self, value, kind=BF16):
         self.value = value
+        self.kind = kind
 
 
 class Far:
@@ -31,59 +32,73 @@
         self.value = value
 
 
-def call(body, outs, *args, scratch=()):
+def call(body, outs, *args, scratch=(), copies=0, limit=VMEM_BYTES):
     place = pl.BlockSpec(memory_space=pltpu.VMEM)
     scalar = pl.BlockSpec(memory_space=pltpu.SMEM)
+    far = pl.BlockSpec(memory_space=pltpu.HBM)
     specs, operands = [], []
     for arg in args:
         if isinstance(arg, Near):
             specs.append(place)
             operands.append(pltpu.with_memory_space_constraint(arg.value, pltpu.VMEM))
         elif isinstance(arg, Far):
-            specs.append(pl.BlockSpec(memory_space=pltpu.HBM))
+            specs.append(far)
             operands.append(pltpu.with_memory_space_constraint(arg.value, pltpu.HBM))
         else:
             specs.append(scalar if arg.dtype == jnp.int32 else place)
             operands.append(arg)
-    shapes = [
-        pltpu.VMEM(out.value, BF16) if isinstance(out, Near) else jax.ShapeDtypeStruct(out, BF16)
-        for out in outs
-    ]
+    shapes, places = [], []
+    for out in outs:
+        if isinstance(out, Near):
+            shapes.append(pltpu.VMEM(out.value, out.kind))
+        elif isinstance(out, Far):
+            shapes.append(pltpu.HBM(out.value, BF16))
+        else:
+            shapes.append(jax.ShapeDtypeStruct(out, BF16))
+        places.append(far if isinstance(out, Far) else place)
+    scratch_shapes = [pltpu.VMEM(shape, BF16) for shape in scratch]
+    if copies:
+        scratch_shapes.append(pltpu.SemaphoreType.DMA((copies,)))
     return pl.pallas_call(
         body,
         out_shape=shapes,
         in_specs=specs,
-        out_specs=[place] * len(outs),
-        scratch_shapes=list(scratch),
-        compiler_params=pltpu.CompilerParams(vmem_limit_bytes=VMEM_BYTES),
+        out_specs=places,
+        scratch_shapes=scratch_shapes,
+        compiler_params=pltpu.CompilerParams(vmem_limit_bytes=limit),
     )(*operands)
 
 
-def load_body(*refs):
-    sources, plain, turned_refs, done = refs[0:4], refs[4:8], refs[8:12], refs[12]
-    copies = [
-        pltpu.make_async_copy(source, target, done.at[i])
-        for i, (source, target) in enumerate(zip(sources, plain))
-    ]
-    for copy in copies:
+class Copies:
+    def __init__(self, done):
+        self.done = done
+        self.count = 0
+
+    def start(self, source, target):
+        copy = pltpu.make_async_copy(source, target, self.done.at[self.count])
+        self.count += 1
         copy.start()
-    for copy, source, target in zip(copies, plain, turned_refs):
-        copy.wait()
+        return copy
+
+
+def load_enter(tokens_far, *refs):
+    sources, plain, turned = refs[0:4], refs[4:8], refs[8:12]
+    x, mixed, tokens, done = refs[12:]
+    copies = Copies(done)
+    came = copies.start(tokens_far, tokens)
+    ready = {}
+    for i in (0, 2, 1, 3):
+        ready[i] = [copies.start(sources[i].at[b], plain[i].at[b]) for b in range(2)]
+    came.wait()
+    x[...] = tokens[...].T
+    for i in (0, 2, 1, 3):
         for b in range(2):
-            target[b] = source[b].T
-
-
-def load(*weights):
-    shapes = [w.shape for w in weights]
-    shapes += [(w.shape[0], w.shape[2], w.shape[1]) for w in weights]
-    return pl.pallas_call(
-        load_body,
-        out_shape=[pltpu.VMEM(shape, BF16) for shape in shapes],
-        in_specs=[pl.BlockSpec(memory_space=pltpu.HBM)] * 4,
-        out_specs=[pl.BlockSpec(memory_space=pltpu.VMEM)] * 8,
-        scratch_shapes=[pltpu.SemaphoreType.DMA((4,))],
-        compiler_params=pltpu.CompilerParams(vmem_limit_bytes=VMEM_BYTES),
-    )(*[pltpu.with_memory_space_constraint(w, pltpu.HBM) for w in weights])
+            ready[i][b].wait()
+            turned[i][b] = plain[i][b].T
+        if i == 0:
+            mixed[...] = interleave(
+                *[dot(turned[0][k], x[256 * k : 256 * (k + 1), :]) for k in range(2)]
+            )
 
 
 def dot(left, right):
@@ -123,11 +138,6 @@
     return a.astype(BF16), b.astype(BF16)
 
 
-def enter(tokens, w1_up, x, mixed):
-    x[...] = tokens[...].T
-    mixed[...] = interleave(*[dot(w1_up[k], x[256 * k : 256 * (k + 1), :]) for k in range(2)])
-
-
 def gelu_tanh(value):
     return jnp.tanh(ROOT * (value + CUBIC * (value * value * value)))
 
@@ -136,30 +146,40 @@
     return 0.5 * value * (1.0 + gelu_tanh(value))
 
 
-def gelu_slope(value):
-    bend = gelu_tanh(value)
+def gelu_slope(value, bend):
     slope = ROOT * (1.0 + 3.0 * CUBIC * (value * value))
     return 0.5 * (1.0 + bend) + (0.5 * value * (1.0 - bend * bend)) * slope
 
 
-def middle(arrived, w2_up, w3_up, spread, *kept):
+def middle(arrived, w2_up, w3_up, spread):
     joined = [half.astype(BF16) for half in halves_of(arrived[...])]
     for g in range(2):
         pre = dot(w2_up[g], joined[g]).astype(BF16)
         act = gelu(pre.astype(F32)).astype(BF16)
-        if kept:
-            kept[0][g] = pre
-            kept[1][g] = act
         out = dot(w3_up[g], act).astype(BF16)
         spread[:, 32 * g : 32 * (g + 1), :] = out.reshape(PEERS, 32, COUNT)
 
 
+def middle_kept(arrived, w2_up, w3_up, spread, slope, mixed_far, act_far, act, done):
+    copies = Copies(done)
+    leaving = [copies.start(arrived, mixed_far)]
+    joined = [half.astype(BF16) for half in halves_of(arrived[...])]
+    for g in range(2):
+        pre = dot(w2_up[g], joined[g]).astype(BF16).astype(F32)
+        bend = gelu_tanh(pre)
+        act[g] = (0.5 * pre * (1.0 + bend)).astype(BF16)
+        leaving.append(copies.start(act.at[g], act_far.at[g]))
+        slope[g] = gelu_slope(pre, bend)
+        out = dot(w3_up[g], act[g]).astype(BF16)
+        spread[:, 32 * g : 32 * (g + 1), :] = out.reshape(PEERS, 32, COUNT)
+    for copy in leaving:
+        copy.wait()
+
+
 def middle_or_first(plane, here, arrived, w2_up, w3_up, far_tokens, w4, spread, up, tokens, done):
     @pl.when(here[0] == plane)
     def _():
-        copy = pltpu.make_async_copy(far_tokens, tokens, done)
-        copy.start()
-        copy.wait()
+        Copies(done).start(far_tokens, tokens).wait()
         up[...] = tokens[...].T
         back_spread(up, w4, spread)
 
@@ -220,52 +240,85 @@
     unmix(arrived[...], w1, up, out)
 
 
-def back_leave(arrived, up, w1, out, parts):
-    for k, part in enumerate(separate(arrived[...])):
-        parts[k] = part
-        rows = slice(256 * k, 256 * (k + 1))
-        total = up[rows, :].astype(F32) + dot(w1[k], part)
-        out[:, rows] = total.astype(BF16).T
-
-
-def back_middle(arrived, pre, w2, w3, back, *kept):
+def back_product(arrived, slope, w2, w3, g):
+    part = arrived[:, 32 * g : 32 * (g + 1), :].reshape(1024, COUNT)
+    grad_pre = (dot(w3[g], part) * slope[g]).astype(BF16)
+    return grad_pre, dot(w2[g], grad_pre)
+
+
+def back_middle(arrived, slope, w2, w3, back):
+    back[...] = stack_halves(*[back_product(arrived, slope, w2, w3, g)[1] for g in range(2)])
+
+
+def back_middle_kept(arrived, slope, w2, w3, back, arrived_far, pre_far, grad_pre, done):
+    copies = Copies(done)
+    leaving = [copies.start(arrived, arrived_far)]
     terms = []
     for g in range(2):
-        part = arrived[:, 32 * g : 32 * (g + 1), :].reshape(1024, COUNT)
-        grad_pre = (dot(w3[g], part) * gelu_slope(pre[g].astype(F32))).astype(BF16)
-        if kept:
-            kept[0][g] = grad_pre
-        terms.append(dot(w2[g], grad_pre))
+        grad_pre[g], term = back_product(arrived, slope, w2, w3, g)
+        leaving.append(copies.start(grad_pre.at[g], pre_far.at[g]))
+        terms.append(term)
     back[...] = stack_halves(*terms)
-
-
-def leave_and_fourth(plane, here, rows_new, rows_held, x, w4_up, up, out, grad):
-    rows = jnp.where(here[0] == plane, rows_new[...], rows_held[...])
-    rows = rows.reshape(64, 32, COUNT)
-    for k in range(2):
-        part = rows[:, 16 * k : 16 * (k + 1), :].reshape(1024, COUNT)
-        place = slice(256 * k, 256 * (k + 1))
-        total = x[place, :].astype(F32) + dot(w4_up[k], part)
-        out[:, place] = total.astype(BF16).T
-        grad[k] = dot_nt(part, up[place, :]).astype(BF16)
-
-
-def grads_third(act, back, grad):
+    for copy in leaving:
+        copy.wait()
+
+
+def gradients(plane, here, *refs):
+    new_in, held_in, x_in, w4_in, up_in, act_in, back_in, mixed_in, pre_in = refs[0:9]
+    out_far, fourth_far, third_far, second_far = refs[9:13]
+    rows, x, w4, up, act, back, mixed, pre, out, fourth, third, second, done = refs[13:]
+    copies = Copies(done)
+    act_ready = copies.start(act_in, act)
+    back_ready = copies.start(back_in, back)
+    ready = [copies.start(mixed_in, mixed), copies.start(pre_in, pre)]
+    ready += [copies.start(x_in, x), copies.start(up_in, up), copies.start(w4_in, w4)]
+    rows_done = done.at[copies.count]
+    copies.count += 1
+
+    @pl.when(here[0] == plane)
+    def _():
+        pltpu.make_async_copy(new_in, rows, rows_done).start()
+
+    @pl.when(here[0] != plane)
+    def _():
+        pltpu.make_async_copy(held_in, rows, rows_done).start()
+
+    leaving = []
+    act_ready.wait()
+    back_ready.wait()
     for g in range(2):
         part = back[:, 32 * g : 32 * (g + 1), :].reshape(1024, COUNT)
-        for start in range(0, 1024, 256):
-            rows = slice(start, start + 256)
-            grad[g, rows, :] = dot_nt(act[g, rows, :], part).astype(BF16)
-
-
-def grads_second(mixed, pre, grad):
+        for half in range(2):
+            band = pl.ds(512 * half, 512)
+            for start in (512 * half, 512 * half + 256):
+                place = slice(start, start + 256)
+                third[g, place, :] = dot_nt(act[g, place, :], part).astype(BF16)
+            leaving.append(copies.start(third.at[g, band], third_far.at[g, band]))
+    for copy in ready:
+        copy.wait()
     for g, part in enumerate(halves_of(mixed[...])):
-        grad[g] = dot_nt(part.astype(BF16), pre[g]).astype(BF16)
-
-
-def grads_first(x, back, grad):
+        second[g] = dot_nt(part.astype(BF16), pre[g]).astype(BF16)
+        leaving.append(copies.start(second.at[g], second_far.at[g]))
+    pltpu.make_async_copy(held_in, rows, rows_done).wait()
+    joined = rows[...].reshape(64, 32, COUNT)
     for k in range(2):
-        grad[k] = dot_nt(x[256 * k : 256 * (k + 1), :], back[k]).astype(BF16)
+        part = joined[:, 16 * k : 16 * (k + 1), :].reshape(1024, COUNT)
+        place = slice(256 * k, 256 * (k + 1))
+        fourth[k] = dot_nt(part, up[place, :]).astype(BF16)
+        leaving.append(copies.start(fourth.at[k], fourth_far.at[k]))
+        total = x[place, :].astype(F32) + dot(w4[k].T, part)
+        out[:, place] = total.astype(BF16).T
+    leaving.append(copies.start(out, out_far))
+    for copy in leaving:
+        copy.wait()
+
+
+def back_leave(arrived, up, w1, x, out, grad):
+    for k, part in enumerate(separate(arrived[...])):
+        place = slice(256 * k, 256 * (k + 1))
+        total = up[place, :].astype(F32) + dot(w1[k], part)
+        out[:, place] = total.astype(BF16).T
+        grad[k] = dot_nt(x[place, :], part).astype(BF16)
 
 
 def exchange(block):
@@ -279,12 +332,20 @@
 
     here = position.astype(jnp.int32).reshape(1)
     tokens, here = lax.optimization_barrier((tokens, here))
-    w1, w2, w3, w4, w1_up, w2_up, w3_up, w4_up = [Near(item) for item in load(*own)]
+    flipped = [(w.shape[0], w.shape[2], w.shape[1]) for w in own]
+    results = call(
+        load_enter,
+        [Near(w.shape) for w in own] + [Near(f) for f in flipped] + [Near(FLAT), Near(CHUNK)],
+        Far(tokens),
+        *[Far(w) for w in own],
+        scratch=[(COUNT, 512)],
+        copies=9,
+    )
+    w1, w2, w3, w4, w1_up, w2_up, w3_up, w4_up = [Near(item) for item in results[:8]]
+    x, mixed = results[8:]
 
     for step in range(segments):
-        if step == 0:
-            x, mixed = call(enter, [Near(FLAT), Near(CHUNK)], tokens, w1_up)
-        else:
+        if step:
             x, mixed = call(
                 functools.partial(enter_choice, step),
                 [Near(FLAT), Near(CHUNK)],
@@ -306,22 +367,25 @@
                 w3_up,
                 Far(cotangent),
                 w4,
-                scratch=[pltpu.VMEM((COUNT, 512), BF16), pltpu.SemaphoreType.DMA],
+                scratch=[(COUNT, 512)],
+                copies=1,
             )
         else:
-            spread, pre, act = call(
-                middle,
-                [Near(WIDE), Near(INNER), Near(INNER)],
+            spread, slope, mixed_in, act = call(
+                middle_kept,
+                [Near(WIDE), Near(INNER, F32), Far(CHUNK), Far(INNER)],
                 Near(arrived),
                 w2_up,
                 w3_up,
+                scratch=[INNER],
+                copies=3,
             )
             break
         rows = exchange(spread)
         (out,) = call(leave, [Near(FLAT)], Near(rows), Near(x), w4_up)
         incoming = lax.ppermute(out, "segment", [(step, step + 1)])
 
-    mixed_in, gathered = arrived, rows
+    gathered = rows
     for step in range(segments):
         last = step == segments - 1
         plane = segments - 1 - step
@@ -346,28 +410,37 @@
                 w4,
             )
             gathered = exchange(spread)
-        shapes = [CHUNK, INNER] if last else [Near(CHUNK)]
-        results = call(back_middle, shapes, Near(gathered), Near(pre), w2, w3)
-        arrived = exchange(results[0])
-        if not last:
-            (grad_in,) = call(back_step, [Near(FLAT)], Near(arrived), Near(up), w1)
-            incoming = lax.ppermute(grad_in, "segment", [(plane, plane - 1)])
-
-    grad_pre = results[1]
-    segment_outputs, fourth_grad = call(
-        functools.partial(leave_and_fourth, segments - 1),
-        [(COUNT, 512), own[3].shape],
+        factors = (Near(gathered), Near(slope), w2, w3)
+        if last:
+            break
+        (back,) = call(back_middle, [Near(CHUNK)], *factors)
+        arrived = exchange(back)
+        (grad_in,) = call(back_step, [Near(FLAT)], Near(arrived), Near(up), w1)
+        incoming = lax.ppermute(grad_in, "segment", [(plane, plane - 1)])
+
+    back, back_spreads, grad_pre = call(
+        back_middle_kept,
+        [CHUNK, Far(WIDE), Far(INNER)],
+        *factors,
+        scratch=[INNER],
+        copies=3,
+    )
+    arrived = exchange(back)
+    far = [Far(item) for item in (rows_last, rows, x, own[3], up, act, back_spreads)]
+    far += [Far(mixed_in), Far(grad_pre)]
+    shapes = [(COUNT, 512), own[3].shape, own[2].shape, own[1].shape]
+    segment_outputs, fourth_grad, third_grad, second_grad = call(
+        functools.partial(gradients, segments - 1),
+        [Far(shape) for shape in shapes],
         here,
-        rows_last,
-        rows,
-        x,
-        w4_up,
-        up,
-    )
-    (third_grad,) = call(grads_third, [own[2].shape], act, gathered)
-    (second_grad,) = call(grads_second, [own[1].shape], mixed_in, grad_pre)
-    grad_in, parts = call(back_leave, [(COUNT, 512), PARTS], arrived, up, own[0])
-    (first_grad,) = call(grads_first, [own[0].shape], x, parts)
+        *far,
+        scratch=[WIDE, FLAT, own[3].shape, FLAT, INNER, WIDE, CHUNK, INNER] + shapes,
+        copies=17,
+        limit=2 * VMEM_BYTES,
+    )
+    grad_in, first_grad = call(
+        back_leave, [(COUNT, 512), own[0].shape], arrived, up, own[0], x
+    )
     return (
         segment_outputs[None],
         grad_in[None],

time: 322 us -> 316 us (0.981)
  local copies, waits for them, and re-layouts: 5.53 us -> 0.03 us
  Pallas kernels: 39.1 us -> 34.7 us
  waiting for transfers between devices: 46.3 us -> 50.2 us
    unnamed x30 -> x14, local copies, waits for them, and re-layouts: 5.53 us -> 0.03 us
    pallas_call x27 -> x23, Pallas kernels: 39.1 us -> 34.7 us  [call(): pl.pallas_call(body, out_shape=shapes, in_specs=specs, out_specs=places,...]
    all_to_all x1, waiting for transfers between devices: 0.01 us -> 3.93 us  [exchange(): return lax.all_to_all(block, 'blk', split_axis=0, concat_axis=0, tiled=True)]
  transfers between devices with their start and end apart: 7 -> 7, of which waited for: 2 -> 3; matrix products, arithmetic and copies ran while one was open for 0% -> 0% of each run, Pallas kernels for 2% -> 2%
where the time goes in v3:
time: 316 us; the launch traced here: 315 us
  blocking collectives  218 us (69%)
  waiting for transfers between devices  50.2 us (16%)
  Pallas kernels  34.7 us (11%)
  starting transfers between devices  11.6 us (4%)
    all_to_all x13, blocking collectives, exchange(): return lax.all_to_all(block, 'blk', split_axis=0, concat_axis=0, tiled=True)  218 us
    ppermute x3, waiting for transfers between devices, shards(): incoming = lax.ppermute(grad_in, 'segment', [(plane, plane - 1)])  41 us
    pallas_call x23, Pallas kernels, call(): pl.pallas_call(body, out_shape=shapes, in_specs=specs, out_specs=places,...  34.7 us
  transfers between devices with their start and end apart: 7, of which 3 were waited for; matrix products, arithmetic and copies ran while one was open for 0% of the time, Pallas kernels for 2%

profile of v3, /device:TPU:1, one launch (start us, length us, event | category | flops | bytes accessed | tf_op | source)
XLA Modules:
  0.0 315.1 jit_solution(5864146129811564579)
XLA Ops:
  0.6 4.0 %shard_map.109 = (bf16[2,256,256]{2,1,0:T(8,128)(2,1)S(1)}, bf16[2,256,1024]{2,1,0:T(8,128)(2,1)S(1)}, bf16[2,1024,1024]{2,1,0:T(8,128)(2,1)S(1)}, bf16[2,1024,2...) custom-call(bf16[256,512]{1,0:T(8,128)(2,1)} %tokens_far, ...), custom_call_target="tpu_custom_call" | custom-call | tf_op jit(solution)/shard_map/pallas_call | solution.py:62
  4.6 17.3 %all_to_all.70.arrived = bf16[32,16,256]{2,1,0:T(8,128)(2,1)S(1)} all-to-all(bf16[32,16,256]{2,1,0:T(8,128)(2,1)S(1)} %get-tuple-element.47), channel_id=1, replica_groups=mesh['segment'=4,'blk'=32] {'blk'}, dimensions={0} | all-to-all | bytes 524288 | tf_op jit(solution)/shard_map/all_to_all | solution.py:325
  21.9 1.8 shard_map.110
  23.7 20.7 %all_to_all.71.arrived = bf16[32,64,256]{2,1,0:T(8,128)(2,1)S(1)} all-to-all(bf16[32,64,256]{2,1,0:T(8,128)(2,1)S(1)} %shard_map.110), channel_id=1, replica_groups=mesh['segment'=4,'blk'=32] {'blk'}, dimensions={0} | all-to-all | bytes 2097152 | tf_op jit(solution)/shard_map/all_to_all | solution.py:325
  44.9 3.6 %collective-permute-start = (bf16[512,256]{1,0:T(8,128)(2,1)S(1)}, bf16[512,256]{1,0:T(8,128)(2,1)S(1)}, u32[]{:S(2)}, u32[]{:S(2)}) collective-permute-start(bf16[512,256]{1,0:T(8,128)(2,1)S(1)} %shard_map.111), channel_id=1, source_target_pairs={{0,32},{1,33},{2,34},{3,35},{4,36},{5,37},{6,38},{7,39},{8,40},{9,... | collective-permute-start | bytes 786440 | tf_op jit(solution)/shard_map/ppermute | solution.py:386
  48.5 5.3 %collective-permute-done.incoming = bf16[512,256]{1,0:T(8,128)(2,1)S(1)} collective-permute-done((bf16[512,256]{1,0:T(8,128)(2,1)S(1)}, bf16[512,256]{1,0:T(8,128)(2,1)S(1)}, u32[]{:S(2)}, u32[]{:S(2)}) %collective-permute-start) | collective-permute-done | bytes 262176 | tf_op jit(solution)/shard_map/ppermute | solution.py:386
  54.0 13.3 %all_to_all.72.arrived = bf16[32,16,256]{2,1,0:T(8,128)(2,1)S(1)} all-to-all(bf16[32,16,256]{2,1,0:T(8,128)(2,1)S(1)} %get-tuple-element.53), channel_id=1, replica_groups=mesh['segment'=4,'blk'=32] {'blk'}, dimensions={0} | all-to-all | bytes 524288 | tf_op jit(solution)/shard_map/all_to_all | solution.py:325
  67.3 1.8 shard_map.113
  69.1 20.7 %all_to_all.73.arrived = bf16[32,64,256]{2,1,0:T(8,128)(2,1)S(1)} all-to-all(bf16[32,64,256]{2,1,0:T(8,128)(2,1)S(1)} %shard_map.113), channel_id=1, replica_groups=mesh['segment'=4,'blk'=32] {'blk'}, dimensions={0} | all-to-all | bytes 2097152 | tf_op jit(solution)/shard_map/all_to_all | solution.py:325
  90.3 0.7 collective-permute-start.1
  91.2 12.4 %all_to_all.74.arrived = bf16[32,16,256]{2,1,0:T(8,128)(2,1)S(1)} all-to-all(bf16[32,16,256]{2,1,0:T(8,128)(2,1)S(1)} %get-tuple-element.55), channel_id=1, replica_groups=mesh['segment'=4,'blk'=32] {'blk'}, dimensions={0} | all-to-all | bytes 524288 | tf_op jit(solution)/shard_map/all_to_all | solution.py:325
  103.7 1.8 shard_map.116
  105.5 20.7 %all_to_all.75.arrived.refs_1_ = bf16[32,64,256]{2,1,0:T(8,128)(2,1)S(1)} all-to-all(bf16[32,64,256]{2,1,0:T(8,128)(2,1)S(1)} %get-tuple-element.57), channel_id=1, replica_groups=mesh['segment'=4,'blk'=32] {'blk'}, dimensions={0} | all-to-all | bytes 2097152 | tf_op jit(solution)/shard_map/all_to_all | solution.py:325
  127.6 12.4 %all_to_all.76.arrived = bf16[32,16,256]{2,1,0:T(8,128)(2,1)S(1)} all-to-all(bf16[32,16,256]{2,1,0:T(8,128)(2,1)S(1)} %get-tuple-element.59), channel_id=1, replica_groups=mesh['segment'=4,'blk'=32] {'blk'}, dimensions={0} | all-to-all | bytes 524288 | tf_op jit(solution)/shard_map/all_to_all | solution.py:325
  140.0 2.6 shard_map.119
  142.7 2.7 shard_map.120
  145.4 12.5 %all_to_all.77.arrived = bf16[32,16,256]{2,1,0:T(8,128)(2,1)S(1)} all-to-all(bf16[32,16,256]{2,1,0:T(8,128)(2,1)S(1)} %shard_map.120), channel_id=1, replica_groups=mesh['segment'=4,'blk'=32] {'blk'}, dimensions={0} | all-to-all | bytes 524288 | tf_op jit(solution)/shard_map/all_to_all | solution.py:325
  158.2 0.7 collective-permute-start.3
  159.3 20.7 %all_to_all.78.arrived.refs_0_ = bf16[32,64,256]{2,1,0:T(8,128)(2,1)S(1)} all-to-all(bf16[32,64,256]{2,1,0:T(8,128)(2,1)S(1)} %get-tuple-element.66), channel_id=1, replica_groups=mesh['segment'=4,'blk'=32] {'blk'}, dimensions={0} | all-to-all | bytes 2097152 | tf_op jit(solution)/shard_map/all_to_all | solution.py:325
  180.1 2.7 shard_map.123
  182.8 12.4 %all_to_all.79.arrived = bf16[32,16,256]{2,1,0:T(8,128)(2,1)S(1)} all-to-all(bf16[32,16,256]{2,1,0:T(8,128)(2,1)S(1)} %shard_map.123), channel_id=1, replica_groups=mesh['segment'=4,'blk'=32] {'blk'}, dimensions={0} | all-to-all | bytes 524288 | tf_op jit(solution)/shard_map/all_to_all | solution.py:325
  196.6 20.7 %all_to_all.80.arrived = bf16[32,64,256]{2,1,0:T(8,128)(2,1)S(1)} all-to-all(bf16[32,64,256]{2,1,0:T(8,128)(2,1)S(1)} %get-tuple-element.69), channel_id=1, replica_groups=mesh['segment'=4,'blk'=32] {'blk'}, dimensions={0} | all-to-all | bytes 2097152 | tf_op jit(solution)/shard_map/all_to_all | solution.py:325
  217.4 2.7 shard_map.126
  220.1 12.4 %all_to_all.81.arrived = bf16[32,16,256]{2,1,0:T(8,128)(2,1)S(1)} all-to-all(bf16[32,16,256]{2,1,0:T(8,128)(2,1)S(1)} %shard_map.126), channel_id=1, replica_groups=mesh['segment'=4,'blk'=32] {'blk'}, dimensions={0} | all-to-all | bytes 524288 | tf_op jit(solution)/shard_map/all_to_all | solution.py:325
  232.8 1.3 collective-permute-start.5
  234.1 41.0 %collective-permute-done.5.incoming = bf16[512,256]{1,0:T(8,128)(2,1)S(1)} collective-permute-done((bf16[512,256]{1,0:T(8,128)(2,1)S(1)}, bf16[512,256]{1,0:T(8,128)(2,1)S(1)}, u32[]{:S(2)}, u32[]{:S(2)}) %collective-permute-start.5) | collective-permute-done | bytes 262176 | tf_op jit(solution)/shard_map/ppermute | solution.py:419
  275.5 21.2 %all_to_all.82.arrived = bf16[32,64,256]{2,1,0:T(8,128)(2,1)S(1)} all-to-all(bf16[32,64,256]{2,1,0:T(8,128)(2,1)S(1)} %get-tuple-element.73), channel_id=1, replica_groups=mesh['segment'=4,'blk'=32] {'blk'}, dimensions={0} | all-to-all | bytes 2097152 | tf_op jit(solution)/shard_map/all_to_all | solution.py:325
  296.7 4.0 %shard_map.129 = (bf16[32,16,256]{2,1,0:T(8,128)(2,1)}, bf16[32,64,256]{2,1,0:T(8,128)(2,1)}, bf16[2,1024,256]{2,1,0:T(8,128)(2,1)}) custom-call(bf16[32,64,256]{2,1,0:T(8,128)(2,1)S(1)} %all_to_all.82.arrived, f32[2,1024,256]{2,1,0:T(8,128)S(1)} %get-tuple-element.61.slope, bf16[2,256,1024]{2,1,0:T(8,128)(2,1)S(1)} %get-tuple-element.62.w2, ...), custom_call_target="tpu_custom_call" | custom-call | tf_op jit(solution)/shard_map/pallas_call | solution.py:62
  300.8 4.1 %all-to-all-start.13 = ((bf16[32,16,256]{2,1,0:T(8,128)(2,1)}), bf16[32,16,256]{2,1,0:T(8,128)(2,1)S(1)}, u32[]{:S(2)}, u32[]{:S(2)}) async-start(bf16[32,16,256]{2,1,0:T(8,128)(2,1)} %get-tuple-element.78), calls=%async_computation.13 | async-start | bytes 524288 | tf_op jit(solution)/shard_map/all_to_all | solution.py:325
  304.9 5.1 %shard_map.130 = (bf16[256,512]{1,0:T(8,128)(2,1)}, bf16[2,1024,256]{2,1,0:T(8,128)(2,1)}, bf16[2,1024,1024]{2,1,0:T(8,128)(2,1)}, bf16[2,256,1024]{2,1,0:T(8,128)(2,1)}) custom-call(s32[1]{0:T(128)} %bitcast.here, bf16[32,64,256]{2,1,0:T(8,128)(2,1)} %copy-done.1, bf16[32,64,256]{2,1,0:T(8,128)(2,1)} %copy-done, bf16[512,256]{1,0:T(8,128)(2,1)} %copy-done.2, ...), custom_call_target="tpu_custom_call" | custom-call | tf_op jit(solution)/shard_map/pallas_call | solution.py:62
  310.0 3.9 %all-to-all-done.13.arrived = bf16[32,16,256]{2,1,0:T(8,128)(2,1)S(1)} async-done(((bf16[32,16,256]{2,1,0:T(8,128)(2,1)}), bf16[32,16,256]{2,1,0:T(8,128)(2,1)S(1)}, u32[]{:S(2)}, u32[]{:S(2)}) %all-to-all-start.13) | async-done | bytes 262176 | tf_op jit(solution)/shard_map/all_to_all | solution.py:325
  313.9 1.2 shard_map.131
  (32 shorter events, 5.6 us)
Async XLA Ops:
  44.9 8.8 %collective-permute-start = (bf16[512,256]{1,0:T(8,128)(2,1)S(1)}, bf16[512,256]{1,0:T(8,128)(2,1)S(1)}, u32[]{:S(2)}, u32[]{:S(2)}) collective-permute-start(bf16[512,256]{1,0:T(8,128)(2,1)S(1)} %shard_map.111), channel_id=1, source_target_pairs={{0,32},{1,33},{2,34},{3,35},{4,36},{5,37},{6,38},{7,39},{8,40},{9,... | collective-permute-start | bytes 786440 | tf_op jit(solution)/shard_map/ppermute | solution.py:386
  90.3 0.7 collective-permute-start.1
  126.2 16.5 %copy-start = (bf16[32,64,256]{2,1,0:T(8,128)(2,1)}, bf16[32,64,256]{2,1,0:T(8,128)(2,1)S(1)}, u32[]{:S(2)}) copy-start(bf16[32,64,256]{2,1,0:T(8,128)(2,1)S(1)} %all_to_all.75.arrived.refs_1_) | copy-start | bytes 3145732
  126.7 0.7 collective-permute-start.2
  127.6 17.8 %copy-start.2 = (bf16[512,256]{1,0:T(8,128)(2,1)}, bf16[512,256]{1,0:T(8,128)(2,1)S(1)}, u32[]{:S(2)}) copy-start(bf16[512,256]{1,0:T(8,128)(2,1)S(1)} %get-tuple-element.67.refs_2_.x) | copy-start | bytes 786436
  158.2 0.7 collective-permute-start.3
  180.1 2.7 copy-start.1
  195.5 0.7 collective-permute-start.4
  232.8 42.3 %collective-permute-start.5 = (bf16[512,256]{1,0:T(8,128)(2,1)S(1)}, bf16[512,256]{1,0:T(8,128)(2,1)S(1)}, u32[]{:S(2)}, u32[]{:S(2)}) collective-permute-start(bf16[512,256]{1,0:T(8,128)(2,1)S(1)} %shard_map.127), channel_id=1, source_target_pairs={{32,0},{33,1},{34,2},{35,3},{36,4},{37,5},{38,6},{39,7},{40,8},{41... | collective-permute-start | bytes 786440 | tf_op jit(solution)/shard_map/ppermute | solution.py:419
  275.5 25.2 %copy-start.4 = (bf16[512,256]{1,0:T(8,128)(2,1)}, bf16[512,256]{1,0:T(8,128)(2,1)S(1)}, u32[]{:S(2)}) copy-start(bf16[512,256]{1,0:T(8,128)(2,1)S(1)} %get-tuple-element.71.refs_4_.up) | copy-start | bytes 786436
  300.8 13.1 %copy-start.3 = (bf16[512,256]{1,0:T(8,128)(2,1)S(1)}, bf16[512,256]{1,0:T(8,128)(2,1)}, u32[]{:S(2)}) copy-start(bf16[512,256]{1,0:T(8,128)(2,1)} %copy-done.2) | copy-start | bytes 786436
  300.8 13.1 %copy-start.6 = (bf16[1,2,256,256]{3,2,1,0:T(8,128)(2,1)S(1)}, bf16[1,2,256,256]{3,2,1,0:T(8,128)(2,1)}, u32[]{:S(2)}) copy-start(bf16[1,2,256,256]{3,2,1,0:T(8,128)(2,1)} %param.8) | copy-start | bytes 786436
  300.8 13.1 %copy-start.5 = (bf16[512,256]{1,0:T(8,128)(2,1)S(1)}, bf16[512,256]{1,0:T(8,128)(2,1)}, u32[]{:S(2)}) copy-start(bf16[512,256]{1,0:T(8,128)(2,1)} %copy-done.4) | copy-start | bytes 786436
  300.8 13.1 %all-to-all-start.13 = ((bf16[32,16,256]{2,1,0:T(8,128)(2,1)}), bf16[32,16,256]{2,1,0:T(8,128)(2,1)S(1)}, u32[]{:S(2)}, u32[]{:S(2)}) async-start(bf16[32,16,256]{2,1,0:T(8,128)(2,1)} %get-tuple-element.78), calls=%async_computation.13 | async-start | bytes 524288 | tf_op jit(solution)/shard_map/all_to_all | solution.py:325

commit v4 on v3

--- a/solution.py
+++ b/solution.py
@@ -151,13 +151,22 @@
     return 0.5 * (1.0 + bend) + (0.5 * value * (1.0 - bend * bend)) * slope
 
 
-def middle(arrived, w2_up, w3_up, spread):
+def middle(arrived, w2_up, w3_up, spread, act):
     joined = [half.astype(BF16) for half in halves_of(arrived[...])]
     for g in range(2):
-        pre = dot(w2_up[g], joined[g]).astype(BF16)
-        act = gelu(pre.astype(F32)).astype(BF16)
-        out = dot(w3_up[g], act).astype(BF16)
-        spread[:, 32 * g : 32 * (g + 1), :] = out.reshape(PEERS, 32, COUNT)
+        for start in range(0, 1024, 256):
+            rows = slice(start, start + 256)
+            pre = dot(w2_up[g, rows, :], joined[g]).astype(BF16)
+            act[g, rows, :] = gelu(pre.astype(F32)).astype(BF16)
+    for g in range(2):
+        spread_rows(w3_up, act, spread, g)
+
+
+def spread_rows(w3_up, act, spread, g):
+    for start in range(0, 1024, 256):
+        out = dot(w3_up[g, start : start + 256, :], act[g]).astype(BF16)
+        peers = slice(start // 32, start // 32 + 8)
+        spread[peers, 32 * g : 32 * (g + 1), :] = out.reshape(8, 32, COUNT)
 
 
 def middle_kept(arrived, w2_up, w3_up, spread, slope, mixed_far, act_far, act, done):
@@ -165,18 +174,20 @@
     leaving = [copies.start(arrived, mixed_far)]
     joined = [half.astype(BF16) for half in halves_of(arrived[...])]
     for g in range(2):
-        pre = dot(w2_up[g], joined[g]).astype(BF16).astype(F32)
-        bend = gelu_tanh(pre)
-        act[g] = (0.5 * pre * (1.0 + bend)).astype(BF16)
+        for start in range(0, 1024, 256):
+            rows = slice(start, start + 256)
+            pre = dot(w2_up[g, rows, :], joined[g]).astype(BF16).astype(F32)
+            bend = gelu_tanh(pre)
+            act[g, rows, :] = (0.5 * pre * (1.0 + bend)).astype(BF16)
+            slope[g, rows, :] = gelu_slope(pre, bend)
         leaving.append(copies.start(act.at[g], act_far.at[g]))
-        slope[g] = gelu_slope(pre, bend)
-        out = dot(w3_up[g], act[g]).astype(BF16)
-        spread[:, 32 * g : 32 * (g + 1), :] = out.reshape(PEERS, 32, COUNT)
+    for g in range(2):
+        spread_rows(w3_up, act, spread, g)
     for copy in leaving:
         copy.wait()
 
 
-def middle_or_first(plane, here, arrived, w2_up, w3_up, far_tokens, w4, spread, up, tokens, done):
+def middle_or_first(plane, here, arrived, w2_up, w3_up, far_tokens, w4, spread, up, tokens, act, done):
     @pl.when(here[0] == plane)
     def _():
         Copies(done).start(far_tokens, tokens).wait()
@@ -186,7 +197,7 @@
     @pl.when(here[0] != plane)
     def _():
         up[...] = jnp.zeros_like(up)
-        middle(arrived, w2_up, w3_up, spread)
+        middle(arrived, w2_up, w3_up, spread, act)
 
 
 def leave_rows(arrived, w4_up, x, out):
@@ -240,25 +251,26 @@
     unmix(arrived[...], w1, up, out)
 
 
-def back_product(arrived, slope, w2, w3, g):
+def back_product(arrived, slope, w3, g, grad_pre):
     part = arrived[:, 32 * g : 32 * (g + 1), :].reshape(1024, COUNT)
-    grad_pre = (dot(w3[g], part) * slope[g]).astype(BF16)
-    return grad_pre, dot(w2[g], grad_pre)
-
-
-def back_middle(arrived, slope, w2, w3, back):
-    back[...] = stack_halves(*[back_product(arrived, slope, w2, w3, g)[1] for g in range(2)])
+    for start in range(0, 1024, 256):
+        rows = slice(start, start + 256)
+        grad_pre[g, rows, :] = (dot(w3[g, rows, :], part) * slope[g, rows, :]).astype(BF16)
+
+
+def back_middle(arrived, slope, w2, w3, back, grad_pre):
+    for g in range(2):
+        back_product(arrived, slope, w3, g, grad_pre)
+    back[...] = stack_halves(*[dot(w2[g], grad_pre[g]) for g in range(2)])
 
 
 def back_middle_kept(arrived, slope, w2, w3, back, arrived_far, pre_far, grad_pre, done):
     copies = Copies(done)
     leaving = [copies.start(arrived, arrived_far)]
-    terms = []
-    for g in range(2):
-        grad_pre[g], term = back_product(arrived, slope, w2, w3, g)
+    for g in range(2):
+        back_product(arrived, slope, w3, g, grad_pre)
         leaving.append(copies.start(grad_pre.at[g], pre_far.at[g]))
-        terms.append(term)
-    back[...] = stack_halves(*terms)
+    back[...] = stack_halves(*[dot(w2[g], grad_pre[g]) for g in range(2)])
     for copy in leaving:
         copy.wait()
 
@@ -356,7 +368,9 @@
             )
         arrived = exchange(mixed)
         if step < segments - 2:
-            (spread,) = call(middle, [Near(WIDE)], Near(arrived), w2_up, w3_up)
+            (spread,) = call(
+                middle, [Near(WIDE)], Near(arrived), w2_up, w3_up, scratch=[INNER]
+            )
         elif step == segments - 2:
             spread, up = call(
                 functools.partial(middle_or_first, segments - 1),
@@ -367,7 +381,7 @@
                 w3_up,
                 Far(cotangent),
                 w4,
-                scratch=[(COUNT, 512)],
+                scratch=[(COUNT, 512), INNER],
                 copies=1,
             )
         else:
@@ -413,7 +427,7 @@
         factors = (Near(gathered), Near(slope), w2, w3)
         if last:
             break
-        (back,) = call(back_middle, [Near(CHUNK)], *factors)
+        (back,) = call(back_middle, [Near(CHUNK)], *factors, scratch=[INNER])
         arrived = exchange(back)
         (grad_in,) = call(back_step, [Near(FLAT)], Near(arrived), Near(up), w1)
         incoming = lax.ppermute(grad_in, "segment", [(plane, plane - 1)])

time: 316 us -> 311 us (0.984)
  Pallas kernels: 34.7 us -> 29.7 us
    pallas_call x23, Pallas kernels: 34.7 us -> 29.7 us  [call(): pl.pallas_call(body, out_shape=shapes, in_specs=specs, out_specs=places,...]
where the time goes in v4:
time: 311 us; the launch traced here: 310 us
  blocking collectives  218 us (70%)
  waiting for transfers between devices  50.2 us (16%)
  Pallas kernels  29.7 us (10%)
  starting transfers between devices  11.6 us (4%)
    all_to_all x13, blocking collectives, exchange(): return lax.all_to_all(block, 'blk', split_axis=0, concat_axis=0, tiled=True)  218 us
    ppermute x3, waiting for transfers between devices, shards(): incoming = lax.ppermute(grad_in, 'segment', [(plane, plane - 1)])  41 us
    pallas_call x23, Pallas kernels, call(): pl.pallas_call(body, out_shape=shapes, in_specs=specs, out_specs=places,...  29.7 us
  transfers between devices with their start and end apart: 7, of which 3 were waited for; matrix products, arithmetic and copies ran while one was open for 0% of the time, Pallas kernels for 2%

profile of v4, /device:TPU:1, one launch (start us, length us, event | category | flops | bytes accessed | tf_op | source)
XLA Modules:
  0.0 310.1 jit_solution(10256783520957161692)
XLA Ops:
  0.6 4.0 %shard_map.109 = (bf16[2,256,256]{2,1,0:T(8,128)(2,1)S(1)}, bf16[2,256,1024]{2,1,0:T(8,128)(2,1)S(1)}, bf16[2,1024,1024]{2,1,0:T(8,128)(2,1)S(1)}, bf16[2,1024,2...) custom-call(bf16[256,512]{1,0:T(8,128)(2,1)} %tokens_far, ...), custom_call_target="tpu_custom_call" | custom-call | tf_op jit(solution)/shard_map/pallas_call | solution.py:62
  4.6 17.3 %all_to_all.70.arrived = bf16[32,16,256]{2,1,0:T(8,128)(2,1)S(1)} all-to-all(bf16[32,16,256]{2,1,0:T(8,128)(2,1)S(1)} %get-tuple-element.47), channel_id=1, replica_groups=mesh['segment'=4,'blk'=32] {'blk'}, dimensions={0} | all-to-all | bytes 524288 | tf_op jit(solution)/shard_map/all_to_all | solution.py:337
  21.9 1.7 shard_map.110
  23.6 20.7 %all_to_all.71.arrived = bf16[32,64,256]{2,1,0:T(8,128)(2,1)S(1)} all-to-all(bf16[32,64,256]{2,1,0:T(8,128)(2,1)S(1)} %shard_map.110), channel_id=1, replica_groups=mesh['segment'=4,'blk'=32] {'blk'}, dimensions={0} | all-to-all | bytes 2097152 | tf_op jit(solution)/shard_map/all_to_all | solution.py:337
  44.8 3.6 %collective-permute-start = (bf16[512,256]{1,0:T(8,128)(2,1)S(1)}, bf16[512,256]{1,0:T(8,128)(2,1)S(1)}, u32[]{:S(2)}, u32[]{:S(2)}) collective-permute-start(bf16[512,256]{1,0:T(8,128)(2,1)S(1)} %shard_map.111), channel_id=1, source_target_pairs={{0,32},{1,33},{2,34},{3,35},{4,36},{5,37},{6,38},{7,39},{8,40},{9,... | collective-permute-start | bytes 786440 | tf_op jit(solution)/shard_map/ppermute | solution.py:400
  48.4 5.3 %collective-permute-done.incoming = bf16[512,256]{1,0:T(8,128)(2,1)S(1)} collective-permute-done((bf16[512,256]{1,0:T(8,128)(2,1)S(1)}, bf16[512,256]{1,0:T(8,128)(2,1)S(1)}, u32[]{:S(2)}, u32[]{:S(2)}) %collective-permute-start) | collective-permute-done | bytes 262176 | tf_op jit(solution)/shard_map/ppermute | solution.py:400
  53.9 13.3 %all_to_all.72.arrived = bf16[32,16,256]{2,1,0:T(8,128)(2,1)S(1)} all-to-all(bf16[32,16,256]{2,1,0:T(8,128)(2,1)S(1)} %get-tuple-element.53), channel_id=1, replica_groups=mesh['segment'=4,'blk'=32] {'blk'}, dimensions={0} | all-to-all | bytes 524288 | tf_op jit(solution)/shard_map/all_to_all | solution.py:337
  67.2 1.7 shard_map.113
  68.9 20.7 %all_to_all.73.arrived = bf16[32,64,256]{2,1,0:T(8,128)(2,1)S(1)} all-to-all(bf16[32,64,256]{2,1,0:T(8,128)(2,1)S(1)} %shard_map.113), channel_id=1, replica_groups=mesh['segment'=4,'blk'=32] {'blk'}, dimensions={0} | all-to-all | bytes 2097152 | tf_op jit(solution)/shard_map/all_to_all | solution.py:337
  90.1 0.7 collective-permute-start.1
  91.0 12.4 %all_to_all.74.arrived = bf16[32,16,256]{2,1,0:T(8,128)(2,1)S(1)} all-to-all(bf16[32,16,256]{2,1,0:T(8,128)(2,1)S(1)} %get-tuple-element.55), channel_id=1, replica_groups=mesh['segment'=4,'blk'=32] {'blk'}, dimensions={0} | all-to-all | bytes 524288 | tf_op jit(solution)/shard_map/all_to_all | solution.py:337
  103.4 1.7 shard_map.116
  105.1 20.7 %all_to_all.75.arrived.refs_1_ = bf16[32,64,256]{2,1,0:T(8,128)(2,1)S(1)} all-to-all(bf16[32,64,256]{2,1,0:T(8,128)(2,1)S(1)} %get-tuple-element.57), channel_id=1, replica_groups=mesh['segment'=4,'blk'=32] {'blk'}, dimensions={0} | all-to-all | bytes 2097152 | tf_op jit(solution)/shard_map/all_to_all | solution.py:337
  126.3 0.7 collective-permute-start.2
  127.3 12.4 %all_to_all.76.arrived = bf16[32,16,256]{2,1,0:T(8,128)(2,1)S(1)} all-to-all(bf16[32,16,256]{2,1,0:T(8,128)(2,1)S(1)} %get-tuple-element.59), channel_id=1, replica_groups=mesh['segment'=4,'blk'=32] {'blk'}, dimensions={0} | all-to-all | bytes 524288 | tf_op jit(solution)/shard_map/all_to_all | solution.py:337
  139.7 2.7 shard_map.119
  142.4 1.6 shard_map.120
  144.0 12.5 %all_to_all.77.arrived = bf16[32,16,256]{2,1,0:T(8,128)(2,1)S(1)} all-to-all(bf16[32,16,256]{2,1,0:T(8,128)(2,1)S(1)} %shard_map.120), channel_id=1, replica_groups=mesh['segment'=4,'blk'=32] {'blk'}, dimensions={0} | all-to-all | bytes 524288 | tf_op jit(solution)/shard_map/all_to_all | solution.py:337
  157.9 20.7 %all_to_all.78.arrived.refs_0_ = bf16[32,64,256]{2,1,0:T(8,128)(2,1)S(1)} all-to-all(bf16[32,64,256]{2,1,0:T(8,128)(2,1)S(1)} %get-tuple-element.66), channel_id=1, replica_groups=mesh['segment'=4,'blk'=32] {'blk'}, dimensions={0} | all-to-all | bytes 2097152 | tf_op jit(solution)/shard_map/all_to_all | solution.py:337
  178.6 1.5 shard_map.123
  180.2 12.4 %all_to_all.79.arrived = bf16[32,16,256]{2,1,0:T(8,128)(2,1)S(1)} all-to-all(bf16[32,16,256]{2,1,0:T(8,128)(2,1)S(1)} %shard_map.123), channel_id=1, replica_groups=mesh['segment'=4,'blk'=32] {'blk'}, dimensions={0} | all-to-all | bytes 524288 | tf_op jit(solution)/shard_map/all_to_all | solution.py:337
  194.1 20.7 %all_to_all.80.arrived = bf16[32,64,256]{2,1,0:T(8,128)(2,1)S(1)} all-to-all(bf16[32,64,256]{2,1,0:T(8,128)(2,1)S(1)} %get-tuple-element.69), channel_id=1, replica_groups=mesh['segment'=4,'blk'=32] {'blk'}, dimensions={0} | all-to-all | bytes 2097152 | tf_op jit(solution)/shard_map/all_to_all | solution.py:337
  214.8 1.5 shard_map.126
  216.4 12.4 %all_to_all.81.arrived = bf16[32,16,256]{2,1,0:T(8,128)(2,1)S(1)} all-to-all(bf16[32,16,256]{2,1,0:T(8,128)(2,1)S(1)} %shard_map.126), channel_id=1, replica_groups=mesh['segment'=4,'blk'=32] {'blk'}, dimensions={0} | all-to-all | bytes 524288 | tf_op jit(solution)/shard_map/all_to_all | solution.py:337
  229.1 1.3 collective-permute-start.5
  230.4 41.0 %collective-permute-done.5.incoming = bf16[512,256]{1,0:T(8,128)(2,1)S(1)} collective-permute-done((bf16[512,256]{1,0:T(8,128)(2,1)S(1)}, bf16[512,256]{1,0:T(8,128)(2,1)S(1)}, u32[]{:S(2)}, u32[]{:S(2)}) %collective-permute-start.5) | collective-permute-done | bytes 262176 | tf_op jit(solution)/shard_map/ppermute | solution.py:433
  271.8 21.2 %all_to_all.82.arrived = bf16[32,64,256]{2,1,0:T(8,128)(2,1)S(1)} all-to-all(bf16[32,64,256]{2,1,0:T(8,128)(2,1)S(1)} %get-tuple-element.73), channel_id=1, replica_groups=mesh['segment'=4,'blk'=32] {'blk'}, dimensions={0} | all-to-all | bytes 2097152 | tf_op jit(solution)/shard_map/all_to_all | solution.py:337
  293.0 2.8 shard_map.129
  295.9 4.1 %all-to-all-start.13 = ((bf16[32,16,256]{2,1,0:T(8,128)(2,1)}), bf16[32,16,256]{2,1,0:T(8,128)(2,1)S(1)}, u32[]{:S(2)}, u32[]{:S(2)}) async-start(bf16[32,16,256]{2,1,0:T(8,128)(2,1)} %get-tuple-element.78), calls=%async_computation.13 | async-start | bytes 524288 | tf_op jit(solution)/shard_map/all_to_all | solution.py:337
  299.9 5.1 %shard_map.130 = (bf16[256,512]{1,0:T(8,128)(2,1)}, bf16[2,1024,256]{2,1,0:T(8,128)(2,1)}, bf16[2,1024,1024]{2,1,0:T(8,128)(2,1)}, bf16[2,256,1024]{2,1,0:T(8,128)(2,1)}) custom-call(s32[1]{0:T(128)} %bitcast.here, bf16[32,64,256]{2,1,0:T(8,128)(2,1)} %copy-done.1, bf16[32,64,256]{2,1,0:T(8,128)(2,1)} %copy-done, bf16[512,256]{1,0:T(8,128)(2,1)} %copy-done.2, ...), custom_call_target="tpu_custom_call" | custom-call | tf_op jit(solution)/shard_map/pallas_call | solution.py:62
  305.0 3.9 %all-to-all-done.13.arrived = bf16[32,16,256]{2,1,0:T(8,128)(2,1)S(1)} async-done(((bf16[32,16,256]{2,1,0:T(8,128)(2,1)}), bf16[32,16,256]{2,1,0:T(8,128)(2,1)S(1)}, u32[]{:S(2)}, u32[]{:S(2)}) %all-to-all-start.13) | async-done | bytes 262176 | tf_op jit(solution)/shard_map/all_to_all | solution.py:337
  309.0 1.2 shard_map.131
  (32 shorter events, 5.7 us)
Async XLA Ops:
  44.8 8.8 %collective-permute-start = (bf16[512,256]{1,0:T(8,128)(2,1)S(1)}, bf16[512,256]{1,0:T(8,128)(2,1)S(1)}, u32[]{:S(2)}, u32[]{:S(2)}) collective-permute-start(bf16[512,256]{1,0:T(8,128)(2,1)S(1)} %shard_map.111), channel_id=1, source_target_pairs={{0,32},{1,33},{2,34},{3,35},{4,36},{5,37},{6,38},{7,39},{8,40},{9,... | collective-permute-start | bytes 786440 | tf_op jit(solution)/shard_map/ppermute | solution.py:400
  90.1 0.7 collective-permute-start.1
  125.9 16.5 %copy-start = (bf16[32,64,256]{2,1,0:T(8,128)(2,1)}, bf16[32,64,256]{2,1,0:T(8,128)(2,1)S(1)}, u32[]{:S(2)}) copy-start(bf16[32,64,256]{2,1,0:T(8,128)(2,1)S(1)} %all_to_all.75.arrived.refs_1_) | copy-start | bytes 3145732
  126.3 0.7 collective-permute-start.2
  127.3 16.7 %copy-start.2 = (bf16[512,256]{1,0:T(8,128)(2,1)}, bf16[512,256]{1,0:T(8,128)(2,1)S(1)}, u32[]{:S(2)}) copy-start(bf16[512,256]{1,0:T(8,128)(2,1)S(1)} %get-tuple-element.67.refs_2_.x) | copy-start | bytes 786436
  156.7 0.7 collective-permute-start.3
  178.6 1.6 copy-start.1
  192.9 0.7 collective-permute-start.4
  229.1 42.3 %collective-permute-start.5 = (bf16[512,256]{1,0:T(8,128)(2,1)S(1)}, bf16[512,256]{1,0:T(8,128)(2,1)S(1)}, u32[]{:S(2)}, u32[]{:S(2)}) collective-permute-start(bf16[512,256]{1,0:T(8,128)(2,1)S(1)} %shard_map.127), channel_id=1, source_target_pairs={{32,0},{33,1},{34,2},{35,3},{36,4},{37,5},{38,6},{39,7},{40,8},{41... | collective-permute-start | bytes 786440 | tf_op jit(solution)/shard_map/ppermute | solution.py:433
  271.8 24.0 %copy-start.4 = (bf16[512,256]{1,0:T(8,128)(2,1)}, bf16[512,256]{1,0:T(8,128)(2,1)S(1)}, u32[]{:S(2)}) copy-start(bf16[512,256]{1,0:T(8,128)(2,1)S(1)} %get-tuple-element.71.refs_4_.up) | copy-start | bytes 786436
  295.8 13.1 %copy-start.3 = (bf16[512,256]{1,0:T(8,128)(2,1)S(1)}, bf16[512,256]{1,0:T(8,128)(2,1)}, u32[]{:S(2)}) copy-start(bf16[512,256]{1,0:T(8,128)(2,1)} %copy-done.2) | copy-start | bytes 786436
  295.8 13.1 %copy-start.6 = (bf16[1,2,256,256]{3,2,1,0:T(8,128)(2,1)S(1)}, bf16[1,2,256,256]{3,2,1,0:T(8,128)(2,1)}, u32[]{:S(2)}) copy-start(bf16[1,2,256,256]{3,2,1,0:T(8,128)(2,1)} %param.8) | copy-start | bytes 786436
  295.9 13.1 %copy-start.5 = (bf16[512,256]{1,0:T(8,128)(2,1)S(1)}, bf16[512,256]{1,0:T(8,128)(2,1)}, u32[]{:S(2)}) copy-start(bf16[512,256]{1,0:T(8,128)(2,1)} %copy-done.4) | copy-start | bytes 786436
  295.9 13.1 %all-to-all-start.13 = ((bf16[32,16,256]{2,1,0:T(8,128)(2,1)}), bf16[32,16,256]{2,1,0:T(8,128)(2,1)S(1)}, u32[]{:S(2)}, u32[]{:S(2)}) async-start(bf16[32,16,256]{2,1,0:T(8,128)(2,1)} %get-tuple-element.78), calls=%async_computation.13 | async-start | bytes 524288 | tf_op jit(solution)/shard_map/all_to_all | solution.py:337

commit v5 on v4

--- a/solution.py
+++ b/solution.py
@@ -169,7 +169,8 @@
         spread[peers, 32 * g : 32 * (g + 1), :] = out.reshape(8, 32, COUNT)
 
 
-def middle_kept(arrived, w2_up, w3_up, spread, slope, mixed_far, act_far, act, done):
+def turn(arrived, gathered, w2_up, w3_up, w2, w3, *refs):
+    spread, slope, mixed_far, act_far, back, act, grad_pre, done = refs
     copies = Copies(done)
     leaving = [copies.start(arrived, mixed_far)]
     joined = [half.astype(BF16) for half in halves_of(arrived[...])]
@@ -183,6 +184,7 @@
         leaving.append(copies.start(act.at[g], act_far.at[g]))
     for g in range(2):
         spread_rows(w3_up, act, spread, g)
+    back_middle(gathered, slope, w2, w3, back, grad_pre)
     for copy in leaving:
         copy.wait()
 
@@ -385,13 +387,16 @@
                 copies=1,
             )
         else:
-            spread, slope, mixed_in, act = call(
-                middle_kept,
-                [Near(WIDE), Near(INNER, F32), Far(CHUNK), Far(INNER)],
+            spread, slope, mixed_in, act, back = call(
+                turn,
+                [Near(WIDE), Near(INNER, F32), Far(CHUNK), Far(INNER), Near(CHUNK)],
                 Near(arrived),
+                Near(rows),
                 w2_up,
                 w3_up,
-                scratch=[INNER],
+                w2,
+                w3,
+                scratch=[INNER, INNER],
                 copies=3,
             )
             break
@@ -399,7 +404,6 @@
         (out,) = call(leave, [Near(FLAT)], Near(rows), Near(x), w4_up)
         incoming = lax.ppermute(out, "segment", [(step, step + 1)])
 
-    gathered = rows
     for step in range(segments):
         last = step == segments - 1
         plane = segments - 1 - step
@@ -424,10 +428,11 @@
                 w4,
             )
             gathered = exchange(spread)
-        factors = (Near(gathered), Near(slope), w2, w3)
-        if last:
-            break
-        (back,) = call(back_middle, [Near(CHUNK)], *factors, scratch=[INNER])
+        if step:
+            factors = (Near(gathered), Near(slope), w2, w3)
+            if last:
+                break
+            (back,) = call(back_middle, [Near(CHUNK)], *factors, scratch=[INNER])
         arrived = exchange(back)
         (grad_in,) = call(back_step, [Near(FLAT)], Near(arrived), Near(up), w1)
         incoming = lax.ppermute(grad_in, "segment", [(plane, plane - 1)])

time: 311 us -> 311 us (level)
    pallas_call x23 -> x22, Pallas kernels: 29.7 us -> 29.6 us  [call(): pl.pallas_call(body, out_shape=shapes, in_specs=specs, out_specs=places,...]
where the time goes in v5:
time: 311 us; the launch traced here: 310 us
  blocking collectives  218 us (70%)
  waiting for transfers between devices  50.2 us (16%)
  Pallas kernels  29.6 us (10%)
  starting transfers between devices  11.6 us (4%)
    all_to_all x13, blocking collectives, exchange(): return lax.all_to_all(block, 'blk', split_axis=0, concat_axis=0, tiled=True)  218 us
    ppermute x3, waiting for transfers between devices, shards(): incoming = lax.ppermute(grad_in, 'segment', [(plane, plane - 1)])  41 us
    pallas_call x22, Pallas kernels, call(): pl.pallas_call(body, out_shape=shapes, in_specs=specs, out_specs=places,...  29.6 us
  transfers between devices with their start and end apart: 7, of which 3 were waited for; matrix products, arithmetic and copies ran while one was open for 0% of the time, Pallas kernels for 2%

profile of v5, /device:TPU:1, one launch (start us, length us, event | category | flops | bytes accessed | tf_op | source)
XLA Modules:
  0.0 309.9 jit_solution(1445351761396843305)
XLA Ops:
  0.6 4.0 %shard_map.109 = (bf16[2,256,256]{2,1,0:T(8,128)(2,1)S(1)}, bf16[2,256,1024]{2,1,0:T(8,128)(2,1)S(1)}, bf16[2,1024,1024]{2,1,0:T(8,128)(2,1)S(1)}, bf16[2,1024,2...) custom-call(bf16[256,512]{1,0:T(8,128)(2,1)} %tokens_far, ...), custom_call_target="tpu_custom_call" | custom-call | tf_op jit(solution)/shard_map/pallas_call | solution.py:62
  4.6 17.3 %all_to_all.70.arrived = bf16[32,16,256]{2,1,0:T(8,128)(2,1)S(1)} all-to-all(bf16[32,16,256]{2,1,0:T(8,128)(2,1)S(1)} %get-tuple-element.48), channel_id=1, replica_groups=mesh['segment'=4,'blk'=32] {'blk'}, dimensions={0} | all-to-all | bytes 524288 | tf_op jit(solution)/shard_map/all_to_all | solution.py:339
  21.9 1.7 shard_map.110
  23.6 20.7 %all_to_all.71.arrived = bf16[32,64,256]{2,1,0:T(8,128)(2,1)S(1)} all-to-all(bf16[32,64,256]{2,1,0:T(8,128)(2,1)S(1)} %shard_map.110), channel_id=1, replica_groups=mesh['segment'=4,'blk'=32] {'blk'}, dimensions={0} | all-to-all | bytes 2097152 | tf_op jit(solution)/shard_map/all_to_all | solution.py:339
  44.8 3.6 %collective-permute-start = (bf16[512,256]{1,0:T(8,128)(2,1)S(1)}, bf16[512,256]{1,0:T(8,128)(2,1)S(1)}, u32[]{:S(2)}, u32[]{:S(2)}) collective-permute-start(bf16[512,256]{1,0:T(8,128)(2,1)S(1)} %shard_map.111), channel_id=1, source_target_pairs={{0,32},{1,33},{2,34},{3,35},{4,36},{5,37},{6,38},{7,39},{8,40},{9,... | collective-permute-start | bytes 786440 | tf_op jit(solution)/shard_map/ppermute | solution.py:405
  48.4 5.3 %collective-permute-done.incoming = bf16[512,256]{1,0:T(8,128)(2,1)S(1)} collective-permute-done((bf16[512,256]{1,0:T(8,128)(2,1)S(1)}, bf16[512,256]{1,0:T(8,128)(2,1)S(1)}, u32[]{:S(2)}, u32[]{:S(2)}) %collective-permute-start) | collective-permute-done | bytes 262176 | tf_op jit(solution)/shard_map/ppermute | solution.py:405
  53.9 13.3 %all_to_all.72.arrived = bf16[32,16,256]{2,1,0:T(8,128)(2,1)S(1)} all-to-all(bf16[32,16,256]{2,1,0:T(8,128)(2,1)S(1)} %get-tuple-element.54), channel_id=1, replica_groups=mesh['segment'=4,'blk'=32] {'blk'}, dimensions={0} | all-to-all | bytes 524288 | tf_op jit(solution)/shard_map/all_to_all | solution.py:339
  67.2 1.7 shard_map.113
  68.9 20.7 %all_to_all.73.arrived = bf16[32,64,256]{2,1,0:T(8,128)(2,1)S(1)} all-to-all(bf16[32,64,256]{2,1,0:T(8,128)(2,1)S(1)} %shard_map.113), channel_id=1, replica_groups=mesh['segment'=4,'blk'=32] {'blk'}, dimensions={0} | all-to-all | bytes 2097152 | tf_op jit(solution)/shard_map/all_to_all | solution.py:339
  90.1 0.7 collective-permute-start.1
  91.0 12.4 %all_to_all.74.arrived = bf16[32,16,256]{2,1,0:T(8,128)(2,1)S(1)} all-to-all(bf16[32,16,256]{2,1,0:T(8,128)(2,1)S(1)} %get-tuple-element.56), channel_id=1, replica_groups=mesh['segment'=4,'blk'=32] {'blk'}, dimensions={0} | all-to-all | bytes 524288 | tf_op jit(solution)/shard_map/all_to_all | solution.py:339
  103.4 1.7 shard_map.116
  105.1 20.7 %all_to_all.75.arrived.gathered.refs_1_ = bf16[32,64,256]{2,1,0:T(8,128)(2,1)S(1)} all-to-all(bf16[32,64,256]{2,1,0:T(8,128)(2,1)S(1)} %get-tuple-element.58), channel_id=1, replica_groups=mesh['segment'=4,'blk'=32] {'blk'}, dimensions={0} | all-to-all | bytes 2097152 | tf_op jit(solution)/shard_map/all_to_all | solution.py:339
  126.3 0.7 collective-permute-start.2
  127.3 12.4 %all_to_all.76.arrived = bf16[32,16,256]{2,1,0:T(8,128)(2,1)S(1)} all-to-all(bf16[32,16,256]{2,1,0:T(8,128)(2,1)S(1)} %get-tuple-element.60), channel_id=1, replica_groups=mesh['segment'=4,'blk'=32] {'blk'}, dimensions={0} | all-to-all | bytes 524288 | tf_op jit(solution)/shard_map/all_to_all | solution.py:339
  139.7 4.1 %shard_map.119 = (bf16[32,64,256]{2,1,0:T(8,128)(2,1)S(1)}, f32[2,1024,256]{2,1,0:T(8,128)S(1)}, bf16[32,16,256]{2,1,0:T(8,128)(2,1)}, bf16[2,1024,256]{2,1,0:T(8,128)(2,1)}, bf16[32,16,256]{2,1,0:T(8,128)(2,1)S(1)}) custom-call(bf16[32,16,256]{2,1,0:T(8,128)(2,1)S(1)} %all_to_all.76.arrived, bf16[32,64,256]{2,1,0:T(8,128)(2,1)S(1)} %all_to_all.75.arrived.gathered.refs_1_, ...), custom_call_target="tpu_custom_call" | custom-call | tf_op jit(solution)/shard_map/pallas_call | solution.py:62
  143.8 12.5 %all_to_all.77.arrived = bf16[32,16,256]{2,1,0:T(8,128)(2,1)S(1)} all-to-all(bf16[32,16,256]{2,1,0:T(8,128)(2,1)S(1)} %get-tuple-element.64), channel_id=1, replica_groups=mesh['segment'=4,'blk'=32] {'blk'}, dimensions={0} | all-to-all | bytes 524288 | tf_op jit(solution)/shard_map/all_to_all | solution.py:339
  157.7 20.7 %all_to_all.78.arrived.refs_0_ = bf16[32,64,256]{2,1,0:T(8,128)(2,1)S(1)} all-to-all(bf16[32,64,256]{2,1,0:T(8,128)(2,1)S(1)} %get-tuple-element.67), channel_id=1, replica_groups=mesh['segment'=4,'blk'=32] {'blk'}, dimensions={0} | all-to-all | bytes 2097152 | tf_op jit(solution)/shard_map/all_to_all | solution.py:339
  178.5 1.5 shard_map.122
  180.0 12.4 %all_to_all.79.arrived = bf16[32,16,256]{2,1,0:T(8,128)(2,1)S(1)} all-to-all(bf16[32,16,256]{2,1,0:T(8,128)(2,1)S(1)} %shard_map.122), channel_id=1, replica_groups=mesh['segment'=4,'blk'=32] {'blk'}, dimensions={0} | all-to-all | bytes 524288 | tf_op jit(solution)/shard_map/all_to_all | solution.py:339
  192.7 0.7 collective-permute-start.4
  193.9 20.7 %all_to_all.80.arrived = bf16[32,64,256]{2,1,0:T(8,128)(2,1)S(1)} all-to-all(bf16[32,64,256]{2,1,0:T(8,128)(2,1)S(1)} %get-tuple-element.71), channel_id=1, replica_groups=mesh['segment'=4,'blk'=32] {'blk'}, dimensions={0} | all-to-all | bytes 2097152 | tf_op jit(solution)/shard_map/all_to_all | solution.py:339
  214.6 1.5 shard_map.125
  216.2 12.4 %all_to_all.81.arrived = bf16[32,16,256]{2,1,0:T(8,128)(2,1)S(1)} all-to-all(bf16[32,16,256]{2,1,0:T(8,128)(2,1)S(1)} %shard_map.125), channel_id=1, replica_groups=mesh['segment'=4,'blk'=32] {'blk'}, dimensions={0} | all-to-all | bytes 524288 | tf_op jit(solution)/shard_map/all_to_all | solution.py:339
  228.9 1.3 collective-permute-start.5
  230.2 41.0 %collective-permute-done.5.incoming = bf16[512,256]{1,0:T(8,128)(2,1)S(1)} collective-permute-done((bf16[512,256]{1,0:T(8,128)(2,1)S(1)}, bf16[512,256]{1,0:T(8,128)(2,1)S(1)}, u32[]{:S(2)}, u32[]{:S(2)}) %collective-permute-start.5) | collective-permute-done | bytes 262176 | tf_op jit(solution)/shard_map/ppermute | solution.py:438
  271.6 21.2 %all_to_all.82.arrived = bf16[32,64,256]{2,1,0:T(8,128)(2,1)S(1)} all-to-all(bf16[32,64,256]{2,1,0:T(8,128)(2,1)S(1)} %get-tuple-element.75), channel_id=1, replica_groups=mesh['segment'=4,'blk'=32] {'blk'}, dimensions={0} | all-to-all | bytes 2097152 | tf_op jit(solution)/shard_map/all_to_all | solution.py:339
  292.8 2.8 shard_map.128
  295.7 4.1 %all-to-all-start.13 = ((bf16[32,16,256]{2,1,0:T(8,128)(2,1)}), bf16[32,16,256]{2,1,0:T(8,128)(2,1)S(1)}, u32[]{:S(2)}, u32[]{:S(2)}) async-start(bf16[32,16,256]{2,1,0:T(8,128)(2,1)} %get-tuple-element.80), calls=%async_computation.13 | async-start | bytes 524288 | tf_op jit(solution)/shard_map/all_to_all | solution.py:339
  299.8 5.1 %shard_map.129 = (bf16[256,512]{1,0:T(8,128)(2,1)}, bf16[2,1024,256]{2,1,0:T(8,128)(2,1)}, bf16[2,1024,1024]{2,1,0:T(8,128)(2,1)}, bf16[2,256,1024]{2,1,0:T(8,128)(2,1)}) custom-call(s32[1]{0:T(128)} %bitcast.here, bf16[32,64,256]{2,1,0:T(8,128)(2,1)} %copy-done.1, bf16[32,64,256]{2,1,0:T(8,128)(2,1)} %copy-done, bf16[512,256]{1,0:T(8,128)(2,1)} %copy-done.2, ...), custom_call_target="tpu_custom_call" | custom-call | tf_op jit(solution)/shard_map/pallas_call | solution.py:62
  304.8 3.9 %all-to-all-done.13.arrived = bf16[32,16,256]{2,1,0:T(8,128)(2,1)S(1)} async-done(((bf16[32,16,256]{2,1,0:T(8,128)(2,1)}), bf16[32,16,256]{2,1,0:T(8,128)(2,1)S(1)}, u32[]{:S(2)}, u32[]{:S(2)}) %all-to-all-start.13) | async-done | bytes 262176 | tf_op jit(solution)/shard_map/all_to_all | solution.py:339
  308.8 1.2 shard_map.130
  (31 shorter events, 5.0 us)
Async XLA Ops:
  44.8 8.8 %collective-permute-start = (bf16[512,256]{1,0:T(8,128)(2,1)S(1)}, bf16[512,256]{1,0:T(8,128)(2,1)S(1)}, u32[]{:S(2)}, u32[]{:S(2)}) collective-permute-start(bf16[512,256]{1,0:T(8,128)(2,1)S(1)} %shard_map.111), channel_id=1, source_target_pairs={{0,32},{1,33},{2,34},{3,35},{4,36},{5,37},{6,38},{7,39},{8,40},{9,... | collective-permute-start | bytes 786440 | tf_op jit(solution)/shard_map/ppermute | solution.py:405
  90.1 0.7 collective-permute-start.1
  125.9 17.9 %copy-start = (bf16[32,64,256]{2,1,0:T(8,128)(2,1)}, bf16[32,64,256]{2,1,0:T(8,128)(2,1)S(1)}, u32[]{:S(2)}) copy-start(bf16[32,64,256]{2,1,0:T(8,128)(2,1)S(1)} %all_to_all.75.arrived.gathered.refs_1_) | copy-start | bytes 3145732
  126.3 0.7 collective-permute-start.2
  127.3 16.5 %copy-start.2 = (bf16[512,256]{1,0:T(8,128)(2,1)}, bf16[512,256]{1,0:T(8,128)(2,1)S(1)}, u32[]{:S(2)}) copy-start(bf16[512,256]{1,0:T(8,128)(2,1)S(1)} %get-tuple-element.68.refs_2_.x) | copy-start | bytes 786436
  156.6 0.7 collective-permute-start.3
  178.4 1.6 copy-start.1
  192.7 0.7 collective-permute-start.4
  228.9 42.3 %collective-permute-start.5 = (bf16[512,256]{1,0:T(8,128)(2,1)S(1)}, bf16[512,256]{1,0:T(8,128)(2,1)S(1)}, u32[]{:S(2)}, u32[]{:S(2)}) collective-permute-start(bf16[512,256]{1,0:T(8,128)(2,1)S(1)} %shard_map.126), channel_id=1, source_target_pairs={{32,0},{33,1},{34,2},{35,3},{36,4},{37,5},{38,6},{39,7},{40,8},{41... | collective-permute-start | bytes 786440 | tf_op jit(solution)/shard_map/ppermute | solution.py:438
  271.6 24.0 %copy-start.4 = (bf16[512,256]{1,0:T(8,128)(2,1)}, bf16[512,256]{1,0:T(8,128)(2,1)S(1)}, u32[]{:S(2)}) copy-start(bf16[512,256]{1,0:T(8,128)(2,1)S(1)} %get-tuple-element.73.refs_4_.up) | copy-start | bytes 786436
  295.7 13.1 %copy-start.3 = (bf16[512,256]{1,0:T(8,128)(2,1)S(1)}, bf16[512,256]{1,0:T(8,128)(2,1)}, u32[]{:S(2)}) copy-start(bf16[512,256]{1,0:T(8,128)(2,1)} %copy-done.2) | copy-start | bytes 786436
  295.7 13.1 %copy-start.6 = (bf16[1,2,256,256]{3,2,1,0:T(8,128)(2,1)S(1)}, bf16[1,2,256,256]{3,2,1,0:T(8,128)(2,1)}, u32[]{:S(2)}) copy-start(bf16[1,2,256,256]{3,2,1,0:T(8,128)(2,1)} %param.8) | copy-start | bytes 786436
  295.7 13.1 %copy-start.5 = (bf16[512,256]{1,0:T(8,128)(2,1)S(1)}, bf16[512,256]{1,0:T(8,128)(2,1)}, u32[]{:S(2)}) copy-start(bf16[512,256]{1,0:T(8,128)(2,1)} %copy-done.4) | copy-start | bytes 786436
  295.7 13.1 %all-to-all-start.13 = ((bf16[32,16,256]{2,1,0:T(8,128)(2,1)}), bf16[32,16,256]{2,1,0:T(8,128)(2,1)S(1)}, u32[]{:S(2)}, u32[]{:S(2)}) async-start(bf16[32,16,256]{2,1,0:T(8,128)(2,1)} %get-tuple-element.80), calls=%async_computation.13 | async-start | bytes 524288 | tf_op jit(solution)/shard_map/all_to_all | solution.py:339
